TPU v7x, 512 devices: a whole 4x8x8 slice. The times are simulated.
512 devices in a mesh: seq: 32 (over x, y), head: 16 (over z, core).
Axes of the slice: x: 4, y: 8, z: 8, core: 2. Of those that a mesh axis runs over, the one named last changes fastest.
Arguments:
- ssm_input: bfloat16 [6144, 16384], P('seq', 'head'), may hold values from -6 to 6
- state_in: bfloat16 [6144, 2048], P('seq'), may hold values from -0.375 to 0.375
- state_out: bfloat16 [6144, 2048], P('seq'), may hold values from -0.078125 to 0.078125
- step_size: float32 [6144, 256], P('seq', 'head'), may hold values from 0.5 to 1.5
- decay_rate: float32 [256], P('head'), may hold values from 8.138021e-06 to 0.04
- forget: float32 [6144], P('seq'), may hold values from 0 to 0.9
- skip_gain: float32 [256], P('head'), may hold values from 0.25 to 1.75
- queries: bfloat16 [6144, 8192], P('seq', 'head'), may hold values from -48 to 48
- new_keys: bfloat16 [6144, 1024], P('seq'), may hold values from -6 to 6
- new_values: bfloat16 [6144, 1024], P('seq'), may hold values from -6 to 6
- cache_keys: bfloat16 [4096, 1024], P('seq'), may hold values from -127 to 127, as said below
- cache_values: bfloat16 [4096, 1024], P('seq'), may hold values from -127 to 127, as said below
- cache_key_scale: float32 [1024], replicated, may hold values from 0.003 to 0.03
- cache_value_scale: float32 [1024], replicated, may hold values from 0.003 to 0.03
Outputs:
- ssm_output: bfloat16 [6144, 16384], P('seq', 'head')
- attended: bfloat16 [6144, 8192], P('seq', 'head')
- key_codes: bfloat16 [6144, 1024], P('seq')
- key_scale: float32 [1024], replicated
Inputs may be any that keep to these rules, and one draw needn't show every extreme that they name: `cache_keys`: whole numbers. `cache_values`: whole numbers.
All inputs are finite; a program needn't handle non-finite values.
Results may differ from a plain program's by a relative error of at most 0.019.
Values may be sent and summed in bfloat16 or wider, within the bound.
No kernel may reach another device: no remote copies, remote signals or barrier semaphores. Data moves between devices by JAX's collectives and lax.ppermute only.
A program may use at most 128 MiB of HBM per device.

v0:
```python
import jax
import jax.numpy as jnp
from jax import lax
from jax.sharding import Mesh
from jax.sharding import PartitionSpec as P

SSM_HEADS = 256
HEAD_DIM = 64
STATE = 256
GROUPS = 8
ATT_HEADS = 64
KV_HEADS = 8
ATT_DIM = 128
SEQ = ("seq_0", "seq_1")


NEG = -1e30


def neutral_like(value, identity):
    return jax.tree.map(
        lambda part, zero: jnp.zeros_like(part) + jnp.asarray(zero, part.dtype), value, identity
    )


def carried_in(value, axes, combine, identity):
    before = start = neutral_like(value, identity)
    running = value
    for axis in reversed(axes):
        devices, mine = (lax.axis_size(axis), lax.axis_index(axis))
        pieces = jax.tree.map(
            lambda part, kind: lax.all_gather(part.astype(kind), axis),
            running,
            (jnp.bfloat16, jnp.bfloat16),
        )
        inside, running = (start, start)
        for k in range(devices):
            passed = k < mine
            running = combine(
                running, jax.tree.map(lambda part, own: part[k].astype(own.dtype), pieces, value)
            )
            inside = jax.tree.map(lambda new, old: jnp.where(passed, new, old), running, inside)
        before = combine(inside, before)
    return before


def in_one_piece(arrays, axis, dim, along):
    both = jnp.concatenate(arrays, axis=along)
    result, at, gathered = (lax.all_gather(both, axis, axis=dim, tiled=True), 0, [])
    for a in arrays:
        gathered.append(lax.slice_in_dim(result, at, at + a.shape[along], axis=along))
        at += a.shape[along]
    return tuple(gathered)


def copy_for_each(value, axis):
    copies = jnp.broadcast_to(value, (lax.axis_size(axis), *value.shape))
    return lax.all_to_all(copies, axis, split_axis=0, concat_axis=0, tiled=True)


def of_everyone(value, axis):
    return copy_for_each(value, axis).max(axis=0)


def head_maps(maps, choose):
    highest = lax.Precision.HIGHEST
    length = maps.shape[0]
    grouped = maps.reshape(length, GROUPS, STATE)
    return jnp.einsum("tgn,hg->thn", grouped, choose, precision=highest)


def span_parts(rate, inputs, in_heads, out_heads):
    highest = lax.Precision.HIGHEST
    length = rate.shape[0]
    lower = jnp.tril(jnp.ones((length, length), jnp.float32))
    running = jnp.dot(lower, rate, precision=highest)
    gram = jnp.einsum("thn,shn->hts", out_heads, in_heads, precision=highest)
    across = running.T
    spread = across[:, :, None] - across[:, None, :]
    causal = lower[None, :, :] > 0.0
    weight = jnp.where(causal, jnp.exp(jnp.where(causal, spread, 0.0)), 0.0) * gram
    within = jnp.einsum("hts,shp->thp", weight, inputs, precision=highest)
    final = running[length - 1]
    tail = jnp.exp(final[None, :] - running)
    local = jnp.einsum("sh,shp,shn->hpn", tail, inputs, in_heads, precision=highest)
    return (running, within, local, jnp.exp(final))


def prior_term(running, out_heads, carried):
    highest = lax.Precision.HIGHEST
    return jnp.exp(running)[:, :, None] * jnp.einsum(
        "thn,hpn->thp", out_heads, carried, precision=highest
    )


def later_state(earlier, later):
    return (earlier[0] * later[0], later[0][:, None, None] * earlier[1] + later[1])


def absorb(carry, q_rows, keys, values, visible):
    peak, total, summed = carry
    count = keys.shape[0]
    groups = q_rows.shape[0]
    width = q_rows.shape[2]
    key_heads = keys.reshape(count, groups, width)
    value_heads = values.reshape(count, groups, width)
    scores = jnp.einsum(
        "grd,kgd->grk", q_rows, key_heads, preferred_element_type=jnp.float32
    ) * width ** (-0.5)
    if visible is not None:
        scores = jnp.where(visible[None], scores, NEG)
    new_peak = jnp.maximum(peak, jnp.max(scores, axis=2))
    weights = jnp.exp(scores - new_peak[:, :, None])
    if visible is not None:
        weights = jnp.where(visible[None], weights, 0.0)
    fade = jnp.exp(peak - new_peak)
    total = fade * total + jnp.sum(weights, axis=2)
    summed = fade[:, :, None] * summed + jnp.einsum(
        "grk,kgd->grd",
        weights.astype(jnp.bfloat16),
        value_heads,
        preferred_element_type=jnp.float32,
    )
    return (new_peak, total, summed)


def absorb_blocks(carry, q_rows, keys, values, placing):
    count = keys.shape[0]
    size = 1024
    blocks = count // size
    key_blocks = keys.reshape(blocks, size, keys.shape[1])
    value_blocks = values.reshape(blocks, size, values.shape[1])

    def advance(state, item):
        key_part, value_part, number = item
        if placing is None:
            visible = None
        else:
            key_pos = number * size + jnp.arange(size, dtype=jnp.int32)
            visible = key_pos[None, :] <= placing[1][:, None]
        return (absorb(state, q_rows, key_part, value_part, visible), None)

    carry, _ = lax.scan(
        advance, carry, (key_blocks, value_blocks, jnp.arange(blocks, dtype=jnp.int32))
    )
    return carry


def body(
    ssm_input,
    state_in,
    state_out,
    step_size,
    decay_rate,
    forget,
    skip_gain,
    queries,
    new_keys,
    new_values,
    cache_keys,
    cache_values,
    cache_key_scale,
    cache_value_scale,
):
    tokens_here = ssm_input.shape[0]
    heads_here = step_size.shape[1]
    rate = -decay_rate[None, :] * step_size - forget[:, None]
    signal = ssm_input.astype(jnp.float32).reshape(tokens_here, heads_here, HEAD_DIM)
    inputs = signal * step_size[:, :, None]
    head_group = (
        lax.axis_index("head") * heads_here + jnp.arange(heads_here, dtype=jnp.int32)
    ) // (SSM_HEADS // GROUPS)
    choose = (head_group[:, None] == jnp.arange(GROUPS, dtype=jnp.int32)[None, :]).astype(
        jnp.float32
    )
    in_heads = head_maps(state_in.astype(jnp.float32), choose)
    out_heads = head_maps(state_out.astype(jnp.float32), choose)
    running, within, local, decay = span_parts(rate, inputs, in_heads, out_heads)
    identity = (jnp.ones_like(decay), jnp.zeros_like(local))
    _, carried = carried_in((decay, local), SEQ, later_state, identity)
    mixed = within + prior_term(running, out_heads, carried) + skip_gain[None, :, None] * signal
    ssm_output = mixed.reshape(tokens_here, heads_here * HEAD_DIM).astype(jnp.bfloat16)
    q_heads = queries.shape[1] // ATT_DIM
    group = ATT_HEADS // KV_HEADS
    kv_here = max(1, q_heads // group)
    share = q_heads // kv_here
    first = lax.axis_index("head") * q_heads // group
    columns = kv_here * ATT_DIM
    key_slice = lax.dynamic_slice_in_dim(cache_keys, first * ATT_DIM, columns, 1)
    value_slice = lax.dynamic_slice_in_dim(cache_values, first * ATT_DIM, columns, 1)
    key_gain = lax.dynamic_slice_in_dim(cache_key_scale, first * ATT_DIM, columns, 0)
    value_gain = lax.dynamic_slice_in_dim(cache_value_scale, first * ATT_DIM, columns, 0)
    cache_k = (key_slice.astype(jnp.float32) * key_gain[None, :]).astype(jnp.bfloat16)
    cache_v = (value_slice.astype(jnp.float32) * value_gain[None, :]).astype(jnp.bfloat16)
    fresh_k = lax.dynamic_slice_in_dim(new_keys, first * ATT_DIM, columns, 1)
    fresh_v = lax.dynamic_slice_in_dim(new_values, first * ATT_DIM, columns, 1)
    row_count = share * tokens_here
    q_rows = (
        queries.reshape(tokens_here, kv_here, share, ATT_DIM)
        .transpose(1, 2, 0, 3)
        .reshape(kv_here, row_count, ATT_DIM)
    )
    empty = (
        jnp.full((kv_here, row_count), NEG, jnp.float32),
        jnp.zeros((kv_here, row_count), jnp.float32),
        jnp.zeros((kv_here, row_count, ATT_DIM), jnp.float32),
    )
    piece = in_one_piece((cache_k, cache_v), SEQ, 0, 1)
    carry = absorb_blocks(empty, q_rows, piece[0], piece[1], None)
    query_pos = (
        lax.axis_index(SEQ) * tokens_here + jnp.arange(row_count, dtype=jnp.int32) % tokens_here
    )
    piece = in_one_piece((fresh_k, fresh_v), SEQ, 0, 1)
    _, total, summed = absorb_blocks(carry, q_rows, piece[0], piece[1], (jnp.int32(0), query_pos))
    result = (summed / total[:, :, None]).astype(jnp.bfloat16)
    attended = (
        result.reshape(kv_here, share, tokens_here, ATT_DIM)
        .transpose(2, 0, 1, 3)
        .reshape(tokens_here, q_heads * ATT_DIM)
    )
    magnitude = jnp.max(jnp.abs(new_keys.astype(jnp.float32)), axis=0)
    magnitude = of_everyone(magnitude, SEQ)
    key_scale = (magnitude + 1e-06) / 127.0
    key_codes = (new_keys.astype(jnp.float32) / key_scale[None, :]).astype(jnp.bfloat16)
    return (ssm_output, attended, key_codes, key_scale)


def solution(mesh):
    split = Mesh(mesh.devices.reshape(4, 8, mesh.shape["head"]), ("seq_0", "seq_1", "head"))
    return jax.shard_map(
        body,
        mesh=split,
        in_specs=(
            P(SEQ, "head"),
            P(SEQ, None),
            P(SEQ, None),
            P(SEQ, "head"),
            P("head"),
            P(SEQ),
            P("head"),
            P(SEQ, "head"),
            P(SEQ, None),
            P(SEQ, None),
            P(SEQ, None),
            P(SEQ, None),
            P(),
            P(),
        ),
        out_specs=(P(SEQ, "head"), P(SEQ, "head"), P(SEQ, None), P()),
        check_vma=False,
    )
```

profile of v0, /device:TPU:1, one launch (start us, length us, event | category | flops | bytes accessed | tf_op | source)
XLA Modules:
  0.0 301.3 jit_solution(2056850521384521667)
XLA Ops:
  13.7 10.6 %all-to-all-start = ((f32[32,1,1024]{2,1,0:T(1,128)}), f32[32,1,1024]{2,1,0:T(1,128)}, u32[]{:S(2)}, u32[]{:S(2)}) async-start(f32[32,1,1024]{2,1,0:T(1,128)} %broadcast_in_dim.96), calls=%async_computation | async-start | bytes 262144 | tf_op jit(solution)/shard_map/all_to_all | solution.py:58
  24.4 2.2 copy.57
  29.0 1.8 convolution_bitcast_fusion
  30.7 5.4 %fusion.88 = bf16[16,64,256]{2,1,0:T(8,128)(2,1)} fusion(f32[192,16,256]{2,1,0:T(8,128)S(1)} %convolution_bitcast_fusion, f32[192,16,64]{0,2,1:T(8,128)S(1)} %bitcast.300, f32[192,16]{0,1:T(8,128)S(1)} %get-tuple-element.208, f32[192,16]{0,1:T(8,128)} %param.21), kind=kOutput, calls=%fused_computation.98 | convolution fusion | flops 604635136 | bytes 4481024 | tf_op jit(solution)/shard_map/sh,shp,shn->hpn/dot_general | solution.py:85
  40.4 1.7 copy-done.1
  42.0 8.2 %fusion.61 = f32[16,192,192]{2,1,0:T(8,128)} fusion(f32[192,16,256]{2,1,0:T(8,128)S(1)} %convolution_bitcast_fusion, f32[192,16,256]{2,1,0:T(8,128)S(1)} %convolution_bitcast_fusion.1), kind=kOutput, calls=%fused_computation.65 | convolution fusion | flops 1811939328 | bytes 8650752 | tf_op jit(solution)/shard_map/thn,shn->hts/dot_general | solution.py:77
  50.3 12.7 %all-gather.1 = bf16[8,1,16]{2,1,0:T(2,128)(2,1)S(1)} all-gather(bf16[1,1,16]{2,1,0:T(2,128)(2,1)} %bitcast.313), channel_id=1, replica_groups=mesh['seq_0'=4,'seq_1'=8,'head'=16] {'seq_1'}, dimensions={0}, use_global_device_ids=true | all-gather | bytes 288 | tf_op jit(solution)/shard_map/all_gather | solution.py:32
  63.0 7.8 %all-gather.2 = bf16[4,1,16]{2,1,0:T(2,128)(2,1)S(1)} all-gather(bf16[1,1,16]{2,1,0:T(2,128)(2,1)S(1)} %fusion.196), channel_id=1, replica_groups=mesh['seq_0'=4,'seq_1'=8,'head'=16] {'seq_0'}, dimensions={0}, use_global_device_ids=true | all-gather | bytes 160 | tf_op jit(solution)/shard_map/all_gather | solution.py:32
  70.8 7.3 %fusion.76 = f32[192,16,64]{0,2,1:T(8,128)} fusion(f32[16,192,192]{2,1,0:T(8,128)} %fusion.61, f32[16,192]{1,0:T(8,128)S(1)} %bitcast.312, pred[192,192]{1,0:T(8,128)(4,1)} %select_compare_fusion, f32[192,16,64]{0,2,1:T(8,128)} %bitcast.299, f32[192,16]{0,1:T(8,128)} %param.21), kind=kOutput, calls=%fused_computation.78 | convolution fusion | flops 455540736 | bytes 3993600 | tf_op jit(solution)/shard_map/hts,shp->thp/dot_general | solution.py:82
  80.2 16.1 %all-gather.10.cloned.1.call-done = bf16[4096,256]{1,0:T(8,128)(2,1)} async-done(((bf16[128,256]{1,0:T(8,128)(2,1)}), bf16[4096,256]{1,0:T(8,128)(2,1)}) %all-gather.10.cloned.1.call-update) | async-done | bytes 2097168 | tf_op jit(solution)/shard_map/all_gather | solution.py:49
  96.3 1.7 fusion.209
  97.9 8.0 %while.31 = (s32[]{:T(128)}, f32[1,768]{1,0:T(1,128)S(1)}, f32[1,768]{1,0:T(1,128)S(1)}, f32[1,768,128]{2,1,0:T(8,128)S(1)}, bf16[4,1024,128]{2,1,0:T(8,128)(2,1...) while((s32[]{:T(128)}, f32[1,768]{1,0:T(1,128)S(1)}, ...), condition=%wide.region_3.4_spmd.clone, body=%wide.region_0.3_spmd.clone.sunk | while | flops 409244160 | bytes 10998905 | solution.py:143
  106.0 76.8 %all-gather.12.cloned.1.call-done = bf16[6144,256]{1,0:T(8,128)(2,1)} async-done(((bf16[192,256]{1,0:T(8,128)(2,1)}), bf16[6144,256]{1,0:T(8,128)(2,1)}) %all-gather.12.cloned.1.call-update) | async-done | bytes 3145744 | tf_op jit(solution)/shard_map/all_gather | solution.py:49
  182.8 3.8 %fusion.208 = (bf16[6144,128]{1,0:T(8,128)(2,1)}, bf16[6144,128]{1,0:T(8,128)(2,1)}) fusion(bf16[6144,256]{1,0:T(8,128)(2,1)} %all-gather.12.cloned.1.call-done), kind=kLoop, calls=%fused_computation.267 | loop fusion | bytes 6291456 | tf_op jit(solution)/shard_map/slice | solution.py:51
  186.6 55.9 %all-gather.14.cloned.1.call-done = bf16[128,64,256]{2,1,0:T(8,128)(2,1)} async-done(((bf16[16,64,256]{2,1,0:T(8,128)(2,1)}), bf16[128,64,256]{2,1,0:T(8,128)(2,1)}) %all-gather.14.cloned.1.call-update) | async-done | bytes 4194320 | tf_op jit(solution)/shard_map/all_gather | solution.py:32
  242.5 4.0 %fusion.134 = bf16[1,16,64,256]{3,2,1,0:T(8,128)(2,1)} fusion(f32[16]{0:T(128)S(1)} %get-tuple-element.210, f32[16]{0:T(128)S(1)} %get-tuple-element.212, f32[16]{0:T(128)S(1)} %get-tuple-element.217, f32[16]{0:T(128)S(1)} %get-tuple-element.216, f32[16]{0:T(128)S(1)} %get-tuple-element.215, f32[16]{0:T(128)S(1)} %get-tuple-element.214, ...), kind=kLoop, calls=%fused_computation.143 | loop fusion | flops 6291456 | bytes 4719104 | tf_op jit(solution)/shard_map/convert_element_type | solution.py:32
  246.6 36.0 %while.30 = (s32[]{:T(128)}, f32[1,768]{1,0:T(1,128)S(1)}, f32[1,768]{1,0:T(1,128)S(1)}, f32[1,768,128]{2,1,0:T(8,128)S(1)}, s32[6]{0:T(128)S(1)}, /*index=5*/bf...) while((s32[]{:T(128)}, f32[1,768]{1,0:T(1,128)S(1)}, ...), condition=%wide.region_7.8_spmd.clone, body=%wide.region_4.7_spmd.clone.sunk | while | flops 415441408 | bytes 11025565 | solution.py:143
  250.4 2.1 fusion.232
  256.3 2.1 fusion.232
  262.3 2.1 fusion.232
  268.3 2.1 fusion.232
  274.2 2.1 fusion.232
  280.1 2.1 fusion.232
  283.6 10.2 %fusion.85 = bf16[192,16,64]{0,2,1:T(8,128)(2,1)S(1)} fusion(f32[192,16,64]{0,2,1:T(8,128)} %fusion.76, f32[192,16,256]{2,1,0:T(8,128)} %copy-done.1, f32[192,16,64]{0,2,1:T(8,128)S(1)} %bitcast.301, bf16[4,16,64,256]{3,2,1,0:T(8,128)(2,1)} %all-gather.8.cloned.1.call-done, f32[16]{0:T(128)S(1)} %copy-done.13, f32[16]{0:T(128)S(1)} %get-tuple-element.210, ...), kind=kOutput, calls=%fused_computation.97 | convolution fusion | flops 617545728 | bytes 11416460 | tf_op jit(solution)/shard_map/thn,hpn->thp/dot_general | solution.py:91
  (147 shorter events, 43.5 us)
Async XLA Ops:
  7.2 3.2 %copy-start = (bf16[192,1024]{1,0:T(8,128)(2,1)S(1)}, bf16[192,1024]{1,0:T(8,128)(2,1)}, u32[]{:S(2)}) copy-start(bf16[192,1024]{1,0:T(8,128)(2,1)} %param.27) | copy-start | bytes 1179652
  7.2 19.4 %copy-start.12 = (f32[16]{0:T(128)S(1)}, f32[16]{0:T(128)}, u32[]{:S(2)}) copy-start(f32[16]{0:T(128)} %param.22) | copy-start | bytes 196
  7.2 19.4 %copy-start.5 = (bf16[192,1024]{1,0:T(8,128)(2,1)S(1)}, bf16[192,1024]{1,0:T(8,128)(2,1)}, u32[]{:S(2)}) copy-start(bf16[192,1024]{1,0:T(8,128)(2,1)} %param.18) | copy-start | bytes 1179652
  7.2 20.6 %copy-start.7 = (f32[192,16]{0,1:T(8,128)S(1)}, f32[192,16]{0,1:T(8,128)}, u32[]{:S(2)}) copy-start(f32[192,16]{0,1:T(8,128)} %param.21) | copy-start | bytes 36868
  7.2 20.6 %copy-start.11 = (f32[192]{0:T(256)S(1)}, f32[192]{0:T(256)}, u32[]{:S(2)}) copy-start(f32[192]{0:T(256)} %param.23) | copy-start | bytes 2308
  7.2 89.0 %all-gather.10.cloned.1.call-start = ((), (), s32[]{:S(2)}) async-start(), calls=%async_computation.2 | async-start | bytes 2162688 | tf_op jit(solution)/shard_map/all_gather | solution.py:49
  10.3 172.4 %all-gather.12.cloned.1.call-start = ((), (), s32[]{:S(2)}) async-start(), calls=%async_computation.3 | async-start | bytes 3244032 | tf_op jit(solution)/shard_map/all_gather | solution.py:49
  13.7 64.6 %all-to-all-start = ((f32[32,1,1024]{2,1,0:T(1,128)}), f32[32,1,1024]{2,1,0:T(1,128)}, u32[]{:S(2)}, u32[]{:S(2)}) async-start(f32[32,1,1024]{2,1,0:T(1,128)} %broadcast_in_dim.96), calls=%async_computation | async-start | bytes 262144 | tf_op jit(solution)/shard_map/all_to_all | solution.py:58
  24.3 218.2 %all-gather.14.cloned.1.call-start = ((), (), s32[]{:S(2)}) async-start(), calls=%async_computation.4 | async-start | bytes 4718592 | tf_op jit(solution)/shard_map/all_gather | solution.py:32
  27.8 2.9 copy-start.2
  27.8 1.1 copy-start.10
  36.1 247.5 %all-gather.8.cloned.1.call-start = ((), (), s32[]{:S(2)}) async-start(), calls=%async_computation.1 | async-start | bytes 2621440 | tf_op jit(solution)/shard_map/all_gather | solution.py:32
  40.3 1.7 copy-start.1
  50.3 27.9 %copy-start.6 = (bf16[192,512]{1,0:T(8,128)(2,1)S(1)}, bf16[192,512]{1,0:T(8,128)(2,1)}, u32[]{:S(2)}) copy-start(bf16[192,512]{1,0:T(8,128)(2,1)} %param.25) | copy-start | bytes 589828
  70.8 8.5 %copy-start.4 = (bf16[192,1024]{1,0:T(8,128)(2,1)S(1)}, bf16[192,1024]{1,0:T(8,128)(2,1)}, u32[]{:S(2)}) copy-start(bf16[192,1024]{1,0:T(8,128)(2,1)} %param.26) | copy-start | bytes 1179652
  79.3 18.6 %copy-start.8 = (f32[1024]{0:T(1024)}, f32[1024]{0:T(1024)S(1)}, u32[]{:S(2)}) copy-start(f32[1024]{0:T(1024)S(1)} %add_multiply_fusion) | copy-start | bytes 12292
  246.5 37.1 %copy-start.3 = (f32[192,1024]{0,1:T(8,128)S(1)}, f32[192,1024]{0,1:T(8,128)}, u32[]{:S(2)}) copy-start(f32[192,1024]{0,1:T(8,128)} %copy.46) | copy-start | bytes 2359300
  246.6 37.1 %copy-start.9 = (f32[192,16]{0,1:T(8,128)S(1)}, f32[192,16]{0,1:T(8,128)}, u32[]{:S(2)}) copy-start(f32[192,16]{0,1:T(8,128)} %get-tuple-element.207) | copy-start | bytes 36868
  246.6 37.1 %copy-start.13 = (f32[16]{0:T(128)S(1)}, f32[16]{0:T(128)}, u32[]{:S(2)}) copy-start(f32[16]{0:T(128)} %param.24) | copy-start | bytes 196
Sparse Core Ops, SparseCore 0:
  11.2 84.9 all-gather.9
  100.0 82.7 all-gather.11
  184.9 57.6 all-gather.13
  246.7 35.1 all-gather.7
where the time goes:
time: 302 us; the launch traced here: 301 us
  waiting for transfers between devices  149 us (49%)
  matrix products  61.9 us (20%)
  local copies, waits for them, and re-layouts  20.8 us (7%)
  blocking collectives  20.5 us (7%)
  other arithmetic  19.3 us (6%)
  between operations  14.1 us (5%)
  starting transfers between devices  11 us (4%)
  loops' own time  4.76 us (2%)
    all_gather x2, waiting for transfers between devices, in_one_piece(): lax.all_gather(both, axis, axis=dim, tiled=True)  92.9 us
    all_gather x2, waiting for transfers between devices, carried_in(): lax.all_gather(part.astype(kind), axis)  55.9 us
    all_gather x2, blocking collectives, carried_in(): lax.all_gather(part.astype(kind), axis)  20.5 us
    dot_general x10, matrix products, absorb(): jnp.einsum('grk,kgd->grd', weights.astype(jnp.bfloat16), value_heads, pre...  15.8 us
    dot_general x10, matrix products, absorb(): jnp.einsum('grd,kgd->grk', q_rows, key_heads, preferred_element_type=jnp....  11.7 us
    all_to_all x1, starting transfers between devices, copy_for_each(): return lax.all_to_all(copies, axis, split_axis=0, concat_axis=0, tiled=True)  10.6 us
    dot_general x1, matrix products, prior_term(): jnp.einsum('thn,hpn->thp', out_heads, carried, precision=highest)  10.2 us
    dot_general x1, matrix products, span_parts(): gram = jnp.einsum('thn,shn->hts', out_heads, in_heads, precision=highest)  8.24 us
  transfers between devices with their start and end apart: 5, of which 3 were waited for; matrix products, arithmetic and copies ran while one was open for 27% of the time, Pallas kernels for 0%

commit v1 on v0

v1 whole, which is shorter than its diff:
```python
import functools

import jax
import jax.numpy as jnp
from jax import lax
from jax.experimental import pallas as pl
from jax.experimental.pallas import tpu as pltpu
from jax.sharding import Mesh
from jax.sharding import PartitionSpec as P

SSM_HEADS = 256
HEAD_DIM = 64
STATE = 256
GROUPS = 8
ATT_HEADS = 64
KV_HEADS = 8
ATT_DIM = 128
SEQ = ("seq_0", "seq_1")
NX, NY, ND = 4, 8, 32

TOK = 192
CROWS = 64
NROWS = 96
HALF = CROWS + NROWS
HEADS = 16
COLS = HEADS * HEAD_DIM
QH = 4
ROWS = QH * TOK
STAT = 32
SLOT = 80
NEG = -1e30
LOG2E = 1.4426950408889634
SCALE = ATT_DIM**-0.5 * LOG2E
F32 = jnp.float32
BF16 = jnp.bfloat16
HIGHEST = lax.Precision.HIGHEST


def whole():
    return pl.BlockSpec(memory_space=pltpu.VMEM)


def call(kernel, out_shape, args, name, flops, scratch=(), moved=1 << 21):
    return pl.pallas_call(
        kernel,
        out_shape=out_shape,
        in_specs=[pl.BlockSpec(memory_space=pltpu.SMEM)] + [whole()] * (len(args) - 1),
        out_specs=jax.tree.map(lambda _: whole(), out_shape),
        scratch_shapes=list(scratch),
        compiler_params=pltpu.CompilerParams(vmem_limit_bytes=56 << 20),
        cost_estimate=pl.CostEstimate(flops=flops, bytes_accessed=moved, transcendentals=0),
        name=name,
    )(*args)


def parts_of(value):
    hi = value.astype(BF16)
    left = value - hi.astype(F32)
    mid = left.astype(BF16)
    low = (left - mid.astype(F32)).astype(BF16)
    return hi, mid, low


def spread_heads(per_head):
    rows = per_head.shape[0]
    low = lax.broadcasted_iota(jnp.int32, (rows, 128), 1) < HEAD_DIM
    tiles = []
    for j in range(HEADS // 2):
        tiles.append(
            jnp.where(low, per_head[:, 2 * j : 2 * j + 1], per_head[:, 2 * j + 1 : 2 * j + 2])
        )
    return jnp.concatenate(tiles, axis=1)


def pack_kernel(place, ck, cv, nk, nv, ks, vs, out):
    keys = (ck[...].astype(F32) * ks[...]).astype(BF16)
    values = (cv[...].astype(F32) * vs[...]).astype(BF16)
    cache = jnp.concatenate([keys, values], axis=1)
    fresh = jnp.concatenate([nk[...], nv[...]], axis=1)
    for k in range(NY):
        out[k, :CROWS, :] = cache
        out[k, CROWS:, :] = fresh


def pack(place, ck, cv, nk, nv, ks, vs):
    row = lambda i, p: (p[3], p[2])
    top = lambda i, p: (0, p[2])
    return pl.pallas_call(
        pack_kernel,
        out_shape=jax.ShapeDtypeStruct((NY, HALF, 2 * ATT_DIM), BF16),
        grid_spec=pltpu.PrefetchScalarGridSpec(
            num_scalar_prefetch=1,
            grid=(1,),
            in_specs=[
                pl.BlockSpec((CROWS, ATT_DIM), row),
                pl.BlockSpec((CROWS, ATT_DIM), row),
                pl.BlockSpec((NROWS, ATT_DIM), row),
                pl.BlockSpec((NROWS, ATT_DIM), row),
                pl.BlockSpec((1, ATT_DIM), top),
                pl.BlockSpec((1, ATT_DIM), top),
            ],
            out_specs=pl.BlockSpec((NY, HALF, 2 * ATT_DIM), lambda i, p: (0, 0, 0)),
        ),
        cost_estimate=pl.CostEstimate(flops=1000000, bytes_accessed=1 << 20, transcendentals=0),
        name="pack",
    )(place, ck, cv, nk, nv, ks, vs)


def local_kernel(place, x, step, b_map, rate_of, forget, nk, send, run_out, run_t_out):
    rows = lax.broadcasted_iota(jnp.int32, (TOK, TOK), 0)
    cols = lax.broadcasted_iota(jnp.int32, (TOK, TOK), 1)
    lost = jnp.sum(jnp.where(rows == cols, forget[...], 0.0), axis=1, keepdims=True)
    rate = -rate_of[...] * step[...] - lost
    lower = (rows >= cols).astype(F32)
    running = jnp.dot(lower, rate, precision=HIGHEST, preferred_element_type=F32)
    run_out[...] = running
    run_t_out[...] = lax.dot_general(
        rate,
        (rows <= cols).astype(F32),
        (((0,), (0,)), ((), ())),
        precision=HIGHEST,
        preferred_element_type=F32,
    )
    final = running[TOK - 1 : TOK, :]
    gain = spread_heads(jnp.exp(final - running) * step[...])
    given = (x[...].astype(F32) * gain).astype(BF16)
    local = lax.dot_general(
        b_map[...], given, (((0,), (0,)), ((), ())), preferred_element_type=F32
    ).astype(BF16)
    decay = spread_heads(jnp.exp(jnp.broadcast_to(final, (8, HEADS))))[0:1, :]
    hi = decay.astype(BF16)
    low = (decay - hi.astype(F32)).astype(BF16)
    peak = jnp.max(jnp.abs(nk[...].astype(F32)), axis=0, keepdims=True)
    blank = jnp.zeros((7, ATT_DIM), F32)
    for d in range(ND):
        block, half = d // 2, d % 2
        tail = []
        for source in (hi, low):
            for j in range(4):
                at = (half * 4 + j) * 128
                tail.append(source[:, at : at + 128].astype(F32))
        tile = d // 4
        tail.append(peak[:, tile * 128 : tile * 128 + 128])
        tail.append(blank)
        for j in range(4):
            at = (half * 4 + j) * 128
            send[d, 16 * j : 16 * j + 16, :] = local[16 * block : 16 * block + 16, at : at + 128]
        send[d, 64:80, :] = jnp.concatenate(tail, axis=0).astype(BF16)


def within_kernel(place, x, step, running, run_t, b_map, c_map, skip, base):
    rows = lax.broadcasted_iota(jnp.int32, (TOK, TOK), 0)
    cols = lax.broadcasted_iota(jnp.int32, (TOK, TOK), 1)
    causal = rows >= cols
    gram = lax.dot_general(
        c_map[...], b_map[...], (((1,), (1,)), ((), ())), preferred_element_type=F32
    )
    signal = x[...].astype(F32)
    given = (signal * spread_heads(step[...])).astype(BF16)
    skips = spread_heads(jnp.broadcast_to(skip[...], (8, HEADS)))[0:1, :]
    low = lax.broadcasted_iota(jnp.int32, (TOK, 128), 1) < HEAD_DIM
    for j in range(HEADS // 2):
        sides = []
        part = given[:, 128 * j : 128 * j + 128]
        for h in (2 * j, 2 * j + 1):
            spread = running[:, h : h + 1] - run_t[h : h + 1, :]
            weight = jnp.exp(jnp.where(causal, spread, NEG)) * gram
            sides.append(jnp.dot(weight.astype(BF16), part, preferred_element_type=F32))
        at = slice(128 * j, 128 * j + 128)
        base[:, at] = jnp.where(low, sides[0], sides[1]) + skips[:, at] * signal[:, at]


def scan_kernel(place, recv, send):
    states = [jnp.zeros((16, 128), F32) for _ in range(4)]
    peak = jnp.max(recv[:, 64:80, :].astype(F32), axis=0)[8:9, :]
    peak = jnp.broadcast_to(peak, (16, 128)).astype(BF16)
    for s in range(ND):
        tail = recv[s, 64:80, :].astype(F32)
        for j in range(4):
            send[s, 16 * j : 16 * j + 16, :] = states[j].astype(BF16)
            decay = tail[j : j + 1, :] + tail[4 + j : 5 + j, :]
            states[j] = decay * states[j] + recv[s, 16 * j : 16 * j + 16, :].astype(F32)
        send[s, 64:80, :] = peak


def final_kernel(place, recv, base, c_map, running, nk, out, codes, scale, carried):
    for d in range(ND):
        block, half = d // 2, d % 2
        for j in range(4):
            at = (half * 4 + j) * 128
            carried[16 * block : 16 * block + 16, at : at + 128] = recv[d, 16 * j : 16 * j + 16, :]
    prior = jnp.dot(c_map[...], carried[...], preferred_element_type=F32)
    out[...] = (base[...] + spread_heads(jnp.exp(running[...])) * prior).astype(BF16)
    peak = jnp.concatenate([recv[4 * t, 64:80, :].astype(F32)[0:1, :] for t in range(8)], axis=1)
    key_scale = (peak + 1e-6) / 127.0
    scale[...] = key_scale
    codes[...] = (nk[...].astype(F32) / key_scale).astype(BF16)


def load_keys(kv_a, kv_b, keys, values):
    at = 0
    for first, count in ((0, CROWS), (CROWS, NROWS)):
        for ref in (kv_a, kv_b):
            size = NY * count
            both = ref[:, first : first + count, :].reshape(size, 2 * ATT_DIM)
            keys[at : at + size, :] = both[:, :ATT_DIM]
            values[at : at + size, :ATT_DIM] = both[:, ATT_DIM:]
            at += size
    values[:, ATT_DIM:] = jnp.ones((NY * 2 * HALF, ATT_DIM), BF16)


CACHED = 2 * NY * CROWS
FRESH = 2 * NY * NROWS


def scores_of(q, keys):
    return lax.dot_general(q, keys, (((1,), (1,)), ((), ())), preferred_element_type=F32)


def attend_kernel(offsets, place, *refs):
    count = len(offsets)
    queries, kv_a, kv_b = refs[:count], refs[count], refs[count + 1]
    outs = refs[count + 2 : 2 * count + 2]
    keys, values, q_rows, sums = refs[2 * count + 2 :]
    mine = place[0]
    load_keys(kv_a, kv_b, keys, values)
    for b in range(count):
        for h in range(QH):
            q_rows[(b * QH + h) * TOK : (b * QH + h + 1) * TOK, :] = queries[b][
                :, h * ATT_DIM : (h + 1) * ATT_DIM
            ]

    def finish(at, summed, top):
        total = summed[:, ATT_DIM:]
        sums[pl.ds(at, TOK), :ATT_DIM] = summed[:, :ATT_DIM] / total
        sums[pl.ds(at, TOK), ATT_DIM:] = top * SCALE + jnp.log2(total)

    def tile(at, owner):
        q = q_rows[pl.ds(at, TOK), :]
        old = scores_of(q, keys[:CACHED, :])
        old_top = jnp.max(old, axis=1, keepdims=True)

        @pl.when(owner < mine)
        def _():
            probs = jnp.exp2(old * SCALE - old_top * SCALE).astype(BF16)
            summed = jnp.dot(probs, values[:CACHED, :], preferred_element_type=F32)
            finish(at, summed, old_top)

        @pl.when(owner >= mine)
        def _():
            new = scores_of(q, keys[CACHED:, :])
            if offsets == (0,):
                col = lax.broadcasted_iota(jnp.int32, (1, FRESH), 1)
                blocks = jnp.zeros((1, FRESH), jnp.int32)
                for k in range(1, 2 * NY):
                    blocks += (col >= k * NROWS).astype(jnp.int32)
                second = (col >= FRESH // 2).astype(jnp.int32)
                side = jnp.where(second == 1, 1 - place[3], place[3])
                pos = col + (blocks + side) * NROWS - second * (2 * NY * NROWS)
                row = lax.broadcasted_iota(jnp.int32, (TOK, 1), 0) + place[1] * TOK
                seen = pos <= row
                new = jnp.where(seen, new, NEG)
            top = jnp.maximum(old_top, jnp.max(new, axis=1, keepdims=True))
            fixed = top * SCALE
            probs = jnp.exp2(old * SCALE - fixed).astype(BF16)
            summed = jnp.dot(probs, values[:CACHED, :], preferred_element_type=F32)
            weights = jnp.exp2(new * SCALE - fixed)
            if offsets == (0,):
                weights = jnp.where(seen, weights, 0.0)
            summed += jnp.dot(
                weights.astype(BF16), values[CACHED:, :], preferred_element_type=F32
            )
            finish(at, summed, top)

    for b in range(count):
        owner = lax.rem(mine + offsets[b] + NX, NX)

        @pl.loop(0, QH)
        def _(h):
            tile(pl.multiple_of((b * QH + h) * TOK, TOK), owner)

    diagonal = lax.broadcasted_iota(jnp.int32, (128, 128), 0) == lax.broadcasted_iota(
        jnp.int32, (128, 128), 1
    )
    for b in range(count):
        outs[b][:ROWS, :] = sums[b * ROWS : (b + 1) * ROWS, :ATT_DIM].astype(BF16)
        lines = []
        for k in range(ROWS // 128):
            block = sums[b * ROWS + k * 128 : b * ROWS + k * 128 + 128, ATT_DIM:]
            lines.append(jnp.sum(jnp.where(diagonal, block, 0.0), axis=0, keepdims=True))
        lines.append(jnp.zeros((2, ATT_DIM), F32))
        stats = jnp.concatenate(lines, axis=0)
        hi, mid, low = parts_of(stats)
        packed = jnp.concatenate(
            [hi.astype(F32), mid.astype(F32), low.astype(F32), jnp.zeros((8, ATT_DIM), F32)], axis=0
        )
        outs[b][ROWS:, :] = packed.astype(BF16)


def attend(place, queries, kv_a, kv_b, offsets, name):
    count = len(offsets)
    partial = jax.ShapeDtypeStruct((ROWS + STAT, ATT_DIM), BF16)
    return call(
        functools.partial(attend_kernel, offsets),
        [partial] * count,
        (place, *queries, kv_a, kv_b),
        name,
        count * 4 * ROWS * (CACHED + FRESH) * ATT_DIM,
        scratch=(
            pltpu.VMEM((CACHED + FRESH, ATT_DIM), BF16),
            pltpu.VMEM((CACHED + FRESH, 2 * ATT_DIM), BF16),
            pltpu.VMEM((count * ROWS, ATT_DIM), BF16),
            pltpu.VMEM((count * ROWS, 2 * ATT_DIM), F32),
        ),
    )


def merge_kernel(place, *refs):
    parts, out = refs[:-1], refs[-1]
    diagonal = lax.broadcasted_iota(jnp.int32, (128, 128), 0) == lax.broadcasted_iota(
        jnp.int32, (128, 128), 1
    )
    stats = []
    for ref in parts:
        packed = ref[ROWS:, :].astype(F32)
        stats.append(packed[0:8] + packed[8:16] + packed[16:24])
    top = functools.reduce(jnp.maximum, stats)
    shares = [jnp.exp2(s - top) for s in stats]
    total = functools.reduce(jnp.add, shares)
    shares = [s / total for s in shares]
    pieces = []
    for k in range(ROWS // 128):
        summed = jnp.zeros((128, 128), F32)
        for share, ref in zip(shares, parts):
            line = jnp.where(diagonal, share[k : k + 1, :], 0.0)
            column = jnp.sum(line, axis=1, keepdims=True)
            summed += column * ref[k * 128 : k * 128 + 128, :].astype(F32)
        pieces.append(summed)
    result = jnp.concatenate(pieces, axis=0)
    for h in range(QH):
        out[:, h * ATT_DIM : (h + 1) * ATT_DIM] = result[h * TOK : (h + 1) * TOK, :].astype(BF16)


def shift(value, axis, by):
    size = lax.axis_size(axis)
    return lax.ppermute(value, axis, [(i, (i + by) % size) for i in range(size)])


def body(
    ssm_input,
    state_in,
    state_out,
    step_size,
    decay_rate,
    forget,
    skip_gain,
    queries,
    new_keys,
    new_values,
    cache_keys,
    cache_values,
    cache_key_scale,
    cache_value_scale,
):
    head = lax.axis_index("head")
    column, core = head // 2, head % 2
    place = jnp.stack(
        [lax.axis_index("seq_0"), lax.axis_index("seq_1"), column, core]
    ).astype(jnp.int32)

    packed = pack(
        place,
        cache_keys,
        cache_values,
        new_keys,
        new_values,
        cache_key_scale.reshape(1, -1),
        cache_value_scale.reshape(1, -1),
    )
    kv_a = lax.all_to_all(packed, "seq_1", 0, 0, tiled=True)
    swap = [(i, i ^ 1) for i in range(lax.axis_size("head"))]
    kv_b = lax.ppermute(kv_a, "head", swap)
    q_left = shift(queries, "seq_0", 1)
    q_right = shift(queries, "seq_0", -1)
    q_far = shift(queries, "seq_0", 2)

    b_map = lax.dynamic_slice_in_dim(state_in, column * STATE, STATE, 1)
    c_map = lax.dynamic_slice_in_dim(state_out, column * STATE, STATE, 1)
    send, running, run_t = call(
        local_kernel,
        [
            jax.ShapeDtypeStruct((ND, SLOT, 128), BF16),
            jax.ShapeDtypeStruct((TOK, HEADS), F32),
            jax.ShapeDtypeStruct((HEADS, TOK), F32),
        ],
        (
            place,
            ssm_input,
            step_size,
            b_map,
            decay_rate.reshape(1, -1),
            forget.reshape(1, -1),
            new_keys,
        ),
        "local",
        2 * TOK * COLS * STATE,
    )
    recv = lax.all_to_all(send, SEQ, 0, 0, tiled=True)
    base = call(
        within_kernel,
        jax.ShapeDtypeStruct((TOK, COLS), F32),
        (place, ssm_input, step_size, running, run_t, b_map, c_map, skip_gain.reshape(1, -1)),
        "within",
        4 * TOK * COLS * TOK,
    )
    back = call(
        scan_kernel,
        jax.ShapeDtypeStruct((ND, SLOT, 128), BF16),
        (place, recv),
        "scan",
        1000000,
    )
    carried = lax.all_to_all(back, SEQ, 0, 0, tiled=True)

    p_left, p_right, p_far = attend(
        place, (q_left, q_right, q_far), kv_a, kv_b, (-1, 1, 2), "attend_others"
    )
    (p_own,) = attend(place, (queries,), kv_a, kv_b, (0,), "attend_own")
    r_left = shift(p_left, "seq_0", -1)
    r_right = shift(p_right, "seq_0", 1)
    r_far = shift(p_far, "seq_0", 2)
    attended = call(
        merge_kernel,
        jax.ShapeDtypeStruct((TOK, QH * ATT_DIM), BF16),
        (place, p_own, r_left, r_right, r_far),
        "merge",
        1000000,
    )
    ssm_output, key_codes, key_scale = call(
        final_kernel,
        [
            jax.ShapeDtypeStruct((TOK, COLS), BF16),
            jax.ShapeDtypeStruct((TOK, KV_HEADS * ATT_DIM), BF16),
            jax.ShapeDtypeStruct((1, KV_HEADS * ATT_DIM), F32),
        ],
        (place, carried, base, c_map, running, new_keys),
        "final",
        2 * TOK * COLS * STATE,
        scratch=(pltpu.VMEM((STATE, COLS), BF16),),
    )
    return (ssm_output, attended, key_codes, key_scale.reshape(-1))


def solution(mesh):
    split = Mesh(mesh.devices.reshape(NX, NY, mesh.shape["head"]), ("seq_0", "seq_1", "head"))
    return jax.shard_map(
        body,
        mesh=split,
        in_specs=(
            P(SEQ, "head"),
            P(SEQ, None),
            P(SEQ, None),
            P(SEQ, "head"),
            P("head"),
            P(SEQ),
            P("head"),
            P(SEQ, "head"),
            P(SEQ, None),
            P(SEQ, None),
            P(SEQ, None),
            P(SEQ, None),
            P(),
            P(),
        ),
        out_specs=(P(SEQ, "head"), P(SEQ, "head"), P(SEQ, None), P()),
        check_vma=False,
    )
```

time: 302 us -> 137 us (0.45)
  waiting for transfers between devices: 149 us -> 40.1 us
  matrix products: 61.9 us -> 0 us
  Pallas kernels: 0 us -> 44.4 us
  starting transfers between devices: 11 us -> 42.9 us
  blocking collectives: 20.5 us -> 0 us
  other arithmetic: 19.3 us -> 0.65 us
  between operations: 14.1 us -> 0.81 us
  local copies, waits for them, and re-layouts: 20.8 us -> 7.53 us
  loops' own time: 4.76 us -> 0 us
    all_gather x4 -> x0, waiting for transfers between devices: 149 us -> none  [the longest x2 92.9 us: in_one_piece(): lax.all_gather(both, axis, axis=dim, tiled=True)]
    dot_general x27 -> x0, matrix products: 61.9 us -> none  [the longest x10 15.8 us: absorb(): jnp.einsum('grk,kgd->grd', weights.astype(jnp.bfloat16), value_heads, pre...]
    pallas_call x0 -> x8, Pallas kernels: none -> 44.4 us  [the longest x7 42.1 us: call(): pl.pallas_call(kernel, out_shape=out_shape, in_specs=[pl.BlockSpec(memory...]
    all_to_all x1 -> x3, waiting for transfers between devices: 0.01 us -> 30.4 us  [the longest x1 16.4 us: body(): kv_a = lax.all_to_all(packed, 'seq_1', 0, 0, tiled=True)]
    ppermute x0 -> x7, starting transfers between devices: none -> 20.5 us  [the longest x6 17.4 us: shift(): lax.ppermute(value, axis, [(i, (i + by) % size) for i in range(size)])]
    all_gather x2 -> x0, blocking collectives: 20.5 us -> none  [carried_in(): lax.all_gather(part.astype(kind), axis)]
    all_to_all x1 -> x3, starting transfers between devices: 10.6 us -> 22.3 us  [the longest x1 10.5 us: body(): recv = lax.all_to_all(send, SEQ, 0, 0, tiled=True)]
    ppermute x0 -> x7, waiting for transfers between devices: none -> 9.67 us  [the longest x6 9.67 us: shift(): lax.ppermute(value, axis, [(i, (i + by) % size) for i in range(size)])]
  transfers between devices with their start and end apart: 5 -> 10, of which waited for: 3 -> 5; matrix products, arithmetic and copies ran while one was open for 27% -> 1% of each run, Pallas kernels for 0% -> 28%
where the time goes in v1:
time: 137 us; the launch traced here: 136 us
  Pallas kernels  44.4 us (32%)
  starting transfers between devices  42.9 us (31%)
  waiting for transfers between devices  40.1 us (29%)
  local copies, waits for them, and re-layouts  7.53 us (5%)
    pallas_call x7, Pallas kernels, call(): pl.pallas_call(kernel, out_shape=out_shape, in_specs=[pl.BlockSpec(memory...  42.1 us
    ppermute x6, starting transfers between devices, shift(): lax.ppermute(value, axis, [(i, (i + by) % size) for i in range(size)])  17.4 us
    all_to_all x1, waiting for transfers between devices, body(): kv_a = lax.all_to_all(packed, 'seq_1', 0, 0, tiled=True)  16.4 us
    all_to_all x1, waiting for transfers between devices, body(): recv = lax.all_to_all(send, SEQ, 0, 0, tiled=True)  14 us
    all_to_all x1, starting transfers between devices, body(): recv = lax.all_to_all(send, SEQ, 0, 0, tiled=True)  10.5 us
    ppermute x6, waiting for transfers between devices, shift(): lax.ppermute(value, axis, [(i, (i + by) % size) for i in range(size)])  9.67 us
    all_to_all x1, starting transfers between devices, body(): kv_a = lax.all_to_all(packed, 'seq_1', 0, 0, tiled=True)  6.39 us
    all_to_all x1, starting transfers between devices, body(): carried = lax.all_to_all(back, SEQ, 0, 0, tiled=True)  5.44 us
  transfers between devices with their start and end apart: 10, of which 5 were waited for; matrix products, arithmetic and copies ran while one was open for 1% of the time, Pallas kernels for 28%

profile of v1, /device:TPU:1, one launch (start us, length us, event | category | flops | bytes accessed | tf_op | source)
XLA Modules:
  0.0 136.4 jit_solution(12346645387601552570)
XLA Ops:
  3.5 3.4 %local.1 = (bf16[32,80,128]{2,1,0:T(8,128)(2,1)}, f32[192,16]{1,0:T(8,128)}, f32[16,192]{1,0:T(8,128)}) custom-call(s32[4]{0:T(128)} %pad_add_fusion.place, bf16[192,1024]{1,0:T(8,128)(2,1)} %x.3, f32[192,16]{1,0:T(8,128)} %copy.18.step, bf16[192,256]{1,0:T(8,128)(2,1)} %constant_dynamic-slice_fusion.1.b_map, f32[1,16]{1,0:T(1,128)} %bitcast.13, ...), custom_call_target="tpu_custom_call" | custom-call | flops 100663296 | bytes 2097152 | tf_op jit(solution)/shard_map/local/pallas_call | solution.py:44
  6.9 10.5 %all-to-all-start = ((bf16[32,80,128]{2,1,0:T(8,128)(2,1)}), bf16[32,80,128]{2,1,0:T(8,128)(2,1)S(1)}, u32[]{:S(2)}, u32[]{:S(2)}) async-start(bf16[32,80,128]{2,1,0:T(8,128)(2,1)} %get-tuple-element.13), calls=%async_computation | async-start | bytes 1310720 | tf_op jit(solution)/shard_map/all_to_all | solution.py:408
  17.4 2.4 %pack.1 = bf16[8,160,256]{2,1,0:T(8,128)(2,1)} custom-call(s32[4]{0:T(128)} %pad_add_fusion.place, bf16[128,1024]{1,0:T(8,128)(2,1)} %ck.1, bf16[128,1024]{1,0:T(8,128)(2,1)} %cv.1, bf16[192,1024]{1,0:T(8,128)(2,1)} %nk.5, bf16[192,1024]{1,0:T(8,128)(2,1)} %nv.1, f32[1,1024]{1,0:T(1,128)} %bitcast.10, f32[1,1024]{1,0:T(1,128)} %bitcast.11), custom_call_target="tpu_custom_call" | custom-call | flops 1000000 | bytes 1048576 | tf_op jit(solution)/shard_map/pack/pallas_call | solution.py:88
  19.8 14.0 %all-to-all-done.recv = bf16[32,80,128]{2,1,0:T(8,128)(2,1)S(1)} async-done(((bf16[32,80,128]{2,1,0:T(8,128)(2,1)}), bf16[32,80,128]{2,1,0:T(8,128)(2,1)S(1)}, u32[]{:S(2)}, u32[]{:S(2)}) %all-to-all-start) | async-done | bytes 655392 | tf_op jit(solution)/shard_map/all_to_all | solution.py:408
  33.8 6.4 %all-to-all-start.2 = ((bf16[8,160,256]{2,1,0:T(8,128)(2,1)}), bf16[8,160,256]{2,1,0:T(8,128)(2,1)S(1)}, u32[]{:S(2)}, u32[]{:S(2)}) async-start(bf16[8,160,256]{2,1,0:T(8,128)(2,1)} %pack.1), calls=%async_computation.2 | async-start | bytes 1310720 | tf_op jit(solution)/shard_map/all_to_all | solution.py:380
  40.2 2.1 %scan.1 = bf16[32,80,128]{2,1,0:T(8,128)(2,1)} custom-call(s32[4]{0:T(128)} %pad_add_fusion.place, bf16[32,80,128]{2,1,0:T(8,128)(2,1)} %copy-done.2), custom_call_target="tpu_custom_call" | custom-call | flops 1000000 | bytes 2097152 | tf_op jit(solution)/shard_map/scan/pallas_call | solution.py:44
  42.3 16.4 %all-to-all-done.2.refs_1_.refs_3_ = bf16[8,160,256]{2,1,0:T(8,128)(2,1)S(1)} async-done(((bf16[8,160,256]{2,1,0:T(8,128)(2,1)}), bf16[8,160,256]{2,1,0:T(8,128)(2,1)S(1)}, u32[]{:S(2)}, u32[]{:S(2)}) %all-to-all-start.2) | async-done | bytes 655392 | tf_op jit(solution)/shard_map/all_to_all | solution.py:380
  58.7 5.4 %all-to-all-start.1 = ((bf16[32,80,128]{2,1,0:T(8,128)(2,1)}), bf16[32,80,128]{2,1,0:T(8,128)(2,1)S(1)}, u32[]{:S(2)}, u32[]{:S(2)}) async-start(bf16[32,80,128]{2,1,0:T(8,128)(2,1)} %scan.1), calls=%async_computation.1 | async-start | bytes 1310720 | tf_op jit(solution)/shard_map/all_to_all | solution.py:423
  64.1 3.2 %collective-permute-start = (bf16[8,160,256]{2,1,0:T(8,128)(2,1)S(1)}, bf16[8,160,256]{2,1,0:T(8,128)(2,1)S(1)}, u32[]{:S(2)}, u32[]{:S(2)}) collective-permute-start(bf16[8,160,256]{2,1,0:T(8,128)(2,1)S(1)} %all-to-all-done.2.refs_1_.refs_3_), channel_id=1, source_target_pairs={{0,1},{1,0},{2,3},{3,2},{4,5},{5,4},{6,7},{7,6},{8,9},{9,8},{10,11... | collective-permute-start | bytes 1966088 | tf_op jit(solution)/shard_map/ppermute | solution.py:382
  67.3 3.4 %collective-permute-start.1 = (bf16[192,512]{1,0:T(8,128)(2,1)S(1)}, bf16[192,512]{1,0:T(8,128)(2,1)S(1)}, u32[]{:S(2)}, u32[]{:S(2)}) collective-permute-start(bf16[192,512]{1,0:T(8,128)(2,1)S(1)} %copy-done.9), channel_id=1, source_target_pairs={{0,128},{128,256},{256,384},{384,0},{1,129},{129,257},{257,385},{3... | collective-permute-start | bytes 589832 | tf_op jit(solution)/shard_map/ppermute | solution.py:346
  70.7 3.2 %collective-permute-start.2 = (bf16[192,512]{1,0:T(8,128)(2,1)S(1)}, bf16[192,512]{1,0:T(8,128)(2,1)S(1)}, u32[]{:S(2)}, u32[]{:S(2)}) collective-permute-start(bf16[192,512]{1,0:T(8,128)(2,1)S(1)} %copy-done.9), channel_id=1, source_target_pairs={{0,384},{128,0},{256,128},{384,256},{1,385},{129,1},{257,129},{385... | collective-permute-start | bytes 589832 | tf_op jit(solution)/shard_map/ppermute | solution.py:346
  73.9 3.6 %collective-permute-start.3 = (bf16[192,512]{1,0:T(8,128)(2,1)S(1)}, bf16[192,512]{1,0:T(8,128)(2,1)S(1)}, u32[]{:S(2)}, u32[]{:S(2)}) collective-permute-start(bf16[192,512]{1,0:T(8,128)(2,1)S(1)} %copy-done.9), channel_id=1, source_target_pairs={{0,256},{128,384},{256,0},{384,128},{1,257},{129,385},{257,1},{385... | collective-permute-start | bytes 589832 | tf_op jit(solution)/shard_map/ppermute | solution.py:346
  77.5 3.6 %collective-permute-done.1.refs_0_ = bf16[192,512]{1,0:T(8,128)(2,1)S(1)} collective-permute-done((bf16[192,512]{1,0:T(8,128)(2,1)S(1)}, bf16[192,512]{1,0:T(8,128)(2,1)S(1)}, u32[]{:S(2)}, u32[]{:S(2)}) %collective-permute-start.1) | collective-permute-done | bytes 196640 | tf_op jit(solution)/shard_map/ppermute | solution.py:346
  81.1 1.7 %collective-permute-done.2.refs_1_ = bf16[192,512]{1,0:T(8,128)(2,1)S(1)} collective-permute-done((bf16[192,512]{1,0:T(8,128)(2,1)S(1)}, bf16[192,512]{1,0:T(8,128)(2,1)S(1)}, u32[]{:S(2)}, u32[]{:S(2)}) %collective-permute-start.2) | collective-permute-done | bytes 196640 | tf_op jit(solution)/shard_map/ppermute | solution.py:346
  82.8 4.4 %collective-permute-done.3.refs_2_ = bf16[192,512]{1,0:T(8,128)(2,1)S(1)} collective-permute-done((bf16[192,512]{1,0:T(8,128)(2,1)S(1)}, bf16[192,512]{1,0:T(8,128)(2,1)S(1)}, u32[]{:S(2)}, u32[]{:S(2)}) %collective-permute-start.3) | collective-permute-done | bytes 196640 | tf_op jit(solution)/shard_map/ppermute | solution.py:346
  88.7 19.5 %attend_others.1 = (bf16[800,128]{1,0:T(8,128)(2,1)}, bf16[800,128]{1,0:T(8,128)(2,1)}, bf16[800,128]{1,0:T(8,128)(2,1)}) custom-call(s32[4]{0:T(128)} %pad_add_fusion.place, bf16[192,512]{1,0:T(8,128)(2,1)} %copy-done.10, bf16[192,512]{1,0:T(8,128)(2,1)} %copy-done.11, bf16[192,512]{1,0:T(8,128)(2,1)} %copy-done.12, bf16[8,160,256]{2,1,0:T(8,128)(2,1)} %copy-done.3, ...), custom_call_target="tpu_custom_call" | custom-call | flops 3019898880 | bytes 2097152 | tf_op jit(solution)/shard_map/attend_others/pallas_call | solution.py:44
  108.3 1.9 %collective-permute-start.4 = (bf16[800,128]{1,0:T(8,128)(2,1)}, bf16[800,128]{1,0:T(8,128)(2,1)S(1)}, u32[]{:S(2)}, u32[]{:S(2)}) collective-permute-start(bf16[800,128]{1,0:T(8,128)(2,1)} %get-tuple-element.17), channel_id=1, source_target_pairs={{0,384},{128,0},{256,128},{384,256},{1,385},{129,1},{257,129},{385... | collective-permute-start | bytes 614408 | tf_op jit(solution)/shard_map/ppermute | solution.py:346
  110.2 3.4 %collective-permute-start.5 = (bf16[800,128]{1,0:T(8,128)(2,1)}, bf16[800,128]{1,0:T(8,128)(2,1)S(1)}, u32[]{:S(2)}, u32[]{:S(2)}) collective-permute-start(bf16[800,128]{1,0:T(8,128)(2,1)} %get-tuple-element.18), channel_id=1, source_target_pairs={{0,128},{128,256},{256,384},{384,0},{1,129},{129,257},{257,385},{3... | collective-permute-start | bytes 614408 | tf_op jit(solution)/shard_map/ppermute | solution.py:346
  113.6 1.9 %collective-permute-start.6 = (bf16[800,128]{1,0:T(8,128)(2,1)}, bf16[800,128]{1,0:T(8,128)(2,1)S(1)}, u32[]{:S(2)}, u32[]{:S(2)}) collective-permute-start(bf16[800,128]{1,0:T(8,128)(2,1)} %get-tuple-element.19), channel_id=1, source_target_pairs={{0,256},{128,384},{256,0},{384,128},{1,257},{129,385},{257,1},{385... | collective-permute-start | bytes 614408 | tf_op jit(solution)/shard_map/ppermute | solution.py:346
  115.5 1.5 %constant_dynamic-slice_fusion.c_map = bf16[192,256]{1,0:T(8,128)(2,1)} fusion(bf16[192,2048]{1,0:T(8,128)(2,1)} %param.16, s32[]{:T(128)S(6)} %select_n.17), kind=kLoop, calls=%fused_computation.1 | loop fusion | bytes 196612 | tf_op jit(solution)/shard_map/dynamic_slice | solution.py:388
  117.0 3.4 %within.1.base = f32[192,1024]{1,0:T(8,128)} custom-call(s32[4]{0:T(128)} %pad_add_fusion.place, bf16[192,1024]{1,0:T(8,128)(2,1)} %x.3, f32[192,16]{1,0:T(8,128)} %copy.18.step, f32[192,16]{1,0:T(8,128)} %get-tuple-element.14.running, f32[16,192]{1,0:T(8,128)} %get-tuple-element.15.run_t, bf16[192,256]{1,0:T(8,128)(2,1)} %constant_dynamic-slice_fusion.1.b_map, ...), custom_call_target="tpu_custom_call" | custom-call | flops 150994944 | bytes 2097152 | tf_op jit(solution)/shard_map/within/pallas_call | solution.py:44
  120.4 8.2 %attend_own.1.refs_0_ = bf16[800,128]{1,0:T(8,128)(2,1)} custom-call(s32[4]{0:T(128)} %pad_add_fusion.place, bf16[192,512]{1,0:T(8,128)(2,1)} %refs_0_.1, bf16[8,160,256]{2,1,0:T(8,128)(2,1)} %copy-done.3, bf16[8,160,256]{2,1,0:T(8,128)(2,1)} %copy-done.8), custom_call_target="tpu_custom_call" | custom-call | flops 1006632960 | bytes 2097152 | tf_op jit(solution)/shard_map/attend_own/pallas_call | solution.py:44
  130.0 2.5 %merge.1 = bf16[192,512]{1,0:T(8,128)(2,1)} custom-call(s32[4]{0:T(128)} %pad_add_fusion.place, bf16[800,128]{1,0:T(8,128)(2,1)} %attend_own.1.refs_0_, bf16[800,128]{1,0:T(8,128)(2,1)} %copy-done.4, bf16[800,128]{1,0:T(8,128)(2,1)} %copy-done.5, bf16[800,128]{1,0:T(8,128)(2,1)} %copy-done.6), custom_call_target="tpu_custom_call" | custom-call | flops 1000000 | bytes 2097152 | tf_op jit(solution)/shard_map/merge/pallas_call | solution.py:44
  133.4 3.0 %final.1 = (bf16[192,1024]{1,0:T(8,128)(2,1)}, bf16[192,1024]{1,0:T(8,128)(2,1)}, f32[1,1024]{1,0:T(1,128)}) custom-call(s32[4]{0:T(128)} %pad_add_fusion.place, bf16[32,80,128]{2,1,0:T(8,128)(2,1)} %copy-done.1, f32[192,1024]{1,0:T(8,128)} %within.1.base, bf16[192,256]{1,0:T(8,128)(2,1)} %constant_dynamic-slice_fusion.c_map, ...), custom_call_target="tpu_custom_call" | custom-call | flops 100663296 | bytes 2097152 | tf_op jit(solution)/shard_map/final/pallas_call | solution.py:44
  (34 shorter events, 6.7 us)
Async XLA Ops:
  0.6 1.6 %copy-start = (bf16[192,2048]{1,0:T(8,128)(2,1)S(1)}, bf16[192,2048]{1,0:T(8,128)(2,1)}, u32[]{:S(2)}) copy-start(bf16[192,2048]{1,0:T(8,128)(2,1)} %param.15) | copy-start | bytes 2359300
  0.7 0.8 copy-start.7
  6.9 26.9 %all-to-all-start = ((bf16[32,80,128]{2,1,0:T(8,128)(2,1)}), bf16[32,80,128]{2,1,0:T(8,128)(2,1)S(1)}, u32[]{:S(2)}, u32[]{:S(2)}) async-start(bf16[32,80,128]{2,1,0:T(8,128)(2,1)} %get-tuple-element.13), calls=%async_computation | async-start | bytes 1310720 | tf_op jit(solution)/shard_map/all_to_all | solution.py:408
  33.8 6.4 %copy-start.2 = (bf16[32,80,128]{2,1,0:T(8,128)(2,1)}, bf16[32,80,128]{2,1,0:T(8,128)(2,1)S(1)}, u32[]{:S(2)}) copy-start(bf16[32,80,128]{2,1,0:T(8,128)(2,1)S(1)} %all-to-all-done.recv) | copy-start | bytes 1966084
  33.8 24.9 %all-to-all-start.2 = ((bf16[8,160,256]{2,1,0:T(8,128)(2,1)}), bf16[8,160,256]{2,1,0:T(8,128)(2,1)S(1)}, u32[]{:S(2)}, u32[]{:S(2)}) async-start(bf16[8,160,256]{2,1,0:T(8,128)(2,1)} %pack.1), calls=%async_computation.2 | async-start | bytes 1310720 | tf_op jit(solution)/shard_map/all_to_all | solution.py:380
  42.3 25.0 %copy-start.9 = (bf16[192,512]{1,0:T(8,128)(2,1)S(1)}, bf16[192,512]{1,0:T(8,128)(2,1)}, u32[]{:S(2)}) copy-start(bf16[192,512]{1,0:T(8,128)(2,1)} %refs_0_.1) | copy-start | bytes 589828
  58.7 5.5 %copy-start.3 = (bf16[8,160,256]{2,1,0:T(8,128)(2,1)}, bf16[8,160,256]{2,1,0:T(8,128)(2,1)S(1)}, u32[]{:S(2)}) copy-start(bf16[8,160,256]{2,1,0:T(8,128)(2,1)S(1)} %all-to-all-done.2.refs_1_.refs_3_) | copy-start | bytes 1966084
  58.7 73.8 %all-to-all-start.1 = ((bf16[32,80,128]{2,1,0:T(8,128)(2,1)}), bf16[32,80,128]{2,1,0:T(8,128)(2,1)S(1)}, u32[]{:S(2)}, u32[]{:S(2)}) async-start(bf16[32,80,128]{2,1,0:T(8,128)(2,1)} %scan.1), calls=%async_computation.1 | async-start | bytes 1310720 | tf_op jit(solution)/shard_map/all_to_all | solution.py:423
  64.1 23.1 %collective-permute-start = (bf16[8,160,256]{2,1,0:T(8,128)(2,1)S(1)}, bf16[8,160,256]{2,1,0:T(8,128)(2,1)S(1)}, u32[]{:S(2)}, u32[]{:S(2)}) collective-permute-start(bf16[8,160,256]{2,1,0:T(8,128)(2,1)S(1)} %all-to-all-done.2.refs_1_.refs_3_), channel_id=1, source_target_pairs={{0,1},{1,0},{2,3},{3,2},{4,5},{5,4},{6,7},{7,6},{8,9},{9,8},{10,11... | collective-permute-start | bytes 1966088 | tf_op jit(solution)/shard_map/ppermute | solution.py:382
  67.3 13.8 %collective-permute-start.1 = (bf16[192,512]{1,0:T(8,128)(2,1)S(1)}, bf16[192,512]{1,0:T(8,128)(2,1)S(1)}, u32[]{:S(2)}, u32[]{:S(2)}) collective-permute-start(bf16[192,512]{1,0:T(8,128)(2,1)S(1)} %copy-done.9), channel_id=1, source_target_pairs={{0,128},{128,256},{256,384},{384,0},{1,129},{129,257},{257,385},{3... | collective-permute-start | bytes 589832 | tf_op jit(solution)/shard_map/ppermute | solution.py:346
  70.7 12.1 %collective-permute-start.2 = (bf16[192,512]{1,0:T(8,128)(2,1)S(1)}, bf16[192,512]{1,0:T(8,128)(2,1)S(1)}, u32[]{:S(2)}, u32[]{:S(2)}) collective-permute-start(bf16[192,512]{1,0:T(8,128)(2,1)S(1)} %copy-done.9), channel_id=1, source_target_pairs={{0,384},{128,0},{256,128},{384,256},{1,385},{129,1},{257,129},{385... | collective-permute-start | bytes 589832 | tf_op jit(solution)/shard_map/ppermute | solution.py:346
  73.9 13.3 %collective-permute-start.3 = (bf16[192,512]{1,0:T(8,128)(2,1)S(1)}, bf16[192,512]{1,0:T(8,128)(2,1)S(1)}, u32[]{:S(2)}, u32[]{:S(2)}) collective-permute-start(bf16[192,512]{1,0:T(8,128)(2,1)S(1)} %copy-done.9), channel_id=1, source_target_pairs={{0,256},{128,384},{256,0},{384,128},{1,257},{129,385},{257,1},{385... | collective-permute-start | bytes 589832 | tf_op jit(solution)/shard_map/ppermute | solution.py:346
  81.1 6.1 %copy-start.10 = (bf16[192,512]{1,0:T(8,128)(2,1)}, bf16[192,512]{1,0:T(8,128)(2,1)S(1)}, u32[]{:S(2)}) copy-start(bf16[192,512]{1,0:T(8,128)(2,1)S(1)} %collective-permute-done.1.refs_0_) | copy-start | bytes 589828
  82.8 4.4 %copy-start.11 = (bf16[192,512]{1,0:T(8,128)(2,1)}, bf16[192,512]{1,0:T(8,128)(2,1)S(1)}, u32[]{:S(2)}) copy-start(bf16[192,512]{1,0:T(8,128)(2,1)S(1)} %collective-permute-done.2.refs_1_) | copy-start | bytes 589828
  87.2 0.7 copy-start.12
  87.9 0.8 copy-start.8
  108.3 20.3 %collective-permute-start.4 = (bf16[800,128]{1,0:T(8,128)(2,1)}, bf16[800,128]{1,0:T(8,128)(2,1)S(1)}, u32[]{:S(2)}, u32[]{:S(2)}) collective-permute-start(bf16[800,128]{1,0:T(8,128)(2,1)} %get-tuple-element.17), channel_id=1, source_target_pairs={{0,384},{128,0},{256,128},{384,256},{1,385},{129,1},{257,129},{385... | collective-permute-start | bytes 614408 | tf_op jit(solution)/shard_map/ppermute | solution.py:346
  110.2 18.4 %collective-permute-start.5 = (bf16[800,128]{1,0:T(8,128)(2,1)}, bf16[800,128]{1,0:T(8,128)(2,1)S(1)}, u32[]{:S(2)}, u32[]{:S(2)}) collective-permute-start(bf16[800,128]{1,0:T(8,128)(2,1)} %get-tuple-element.18), channel_id=1, source_target_pairs={{0,128},{128,256},{256,384},{384,0},{1,129},{129,257},{257,385},{3... | collective-permute-start | bytes 614408 | tf_op jit(solution)/shard_map/ppermute | solution.py:346
  113.6 15.1 %collective-permute-start.6 = (bf16[800,128]{1,0:T(8,128)(2,1)}, bf16[800,128]{1,0:T(8,128)(2,1)S(1)}, u32[]{:S(2)}, u32[]{:S(2)}) collective-permute-start(bf16[800,128]{1,0:T(8,128)(2,1)} %get-tuple-element.19), channel_id=1, source_target_pairs={{0,256},{128,384},{256,0},{384,128},{1,257},{129,385},{257,1},{385... | collective-permute-start | bytes 614408 | tf_op jit(solution)/shard_map/ppermute | solution.py:346
  128.6 0.7 copy-start.4
  128.6 0.7 copy-start.5
  129.3 0.7 copy-start.6
  132.5 0.9 copy-start.1

commit v2 on v1

v2 whole, which is shorter than its diff:
```python
import functools

import jax
import jax.numpy as jnp
from jax import lax
from jax.experimental import pallas as pl
from jax.experimental.pallas import tpu as pltpu
from jax.sharding import Mesh
from jax.sharding import PartitionSpec as P

SSM_HEADS = 256
HEAD_DIM = 64
STATE = 256
GROUPS = 8
ATT_HEADS = 64
KV_HEADS = 8
ATT_DIM = 128
SEQ = ("seq_0", "seq_1")
NX, NY, ND = 4, 8, 32

TOK = 192
CROWS = 64
NROWS = 96
HALF = CROWS + NROWS
HEADS = 16
COLS = HEADS * HEAD_DIM
QH = 4
ROWS = QH * TOK
STAT = 32
SENT = CROWS + NROWS + 16
SLOT = 72
BACK = 64
NEG = -1e30
LOG2E = 1.4426950408889634
SCALE = ATT_DIM**-0.5 * LOG2E
F32 = jnp.float32
BF16 = jnp.bfloat16
LIMIT = 24 << 20
HIGHEST = lax.Precision.HIGHEST


def whole():
    return pl.BlockSpec(memory_space=pltpu.VMEM)


def call(kernel, out_shape, args, name, flops, scratch=(), moved=1 << 21, after=()):
    def inner(*refs):
        kernel(*refs[: len(args)], *refs[len(args) + len(after) :])

    return pl.pallas_call(
        inner,
        out_shape=out_shape,
        in_specs=[pl.BlockSpec(memory_space=pltpu.SMEM)] + [whole()] * (len(args) - 1)
        + [whole()] * len(after),
        out_specs=jax.tree.map(lambda _: whole(), out_shape),
        scratch_shapes=list(scratch),
        compiler_params=pltpu.CompilerParams(vmem_limit_bytes=LIMIT),
        cost_estimate=pl.CostEstimate(flops=flops, bytes_accessed=moved, transcendentals=0),
        name=name,
    )(*args, *after)


def parts_of(value):
    hi = value.astype(BF16)
    left = value - hi.astype(F32)
    mid = left.astype(BF16)
    low = (left - mid.astype(F32)).astype(BF16)
    return hi, mid, low


def hold(value, after):
    return pl.pallas_call(
        lambda *refs: None,
        out_shape=jax.ShapeDtypeStruct(value.shape, value.dtype),
        in_specs=[pl.BlockSpec(memory_space=pl.ANY)] * (1 + len(after)),
        out_specs=pl.BlockSpec(memory_space=pl.ANY),
        input_output_aliases={0: 0},
        compiler_params=pltpu.CompilerParams(vmem_limit_bytes=LIMIT),
        name="hold",
    )(value, *after)


def spread_heads(per_head):
    rows = per_head.shape[0]
    low = lax.broadcasted_iota(jnp.int32, (rows, 128), 1) < HEAD_DIM
    tiles = []
    for j in range(HEADS // 2):
        tiles.append(
            jnp.where(low, per_head[:, 2 * j : 2 * j + 1], per_head[:, 2 * j + 1 : 2 * j + 2])
        )
    return jnp.concatenate(tiles, axis=1)


def pack_kernel(place, ck, cv, nk, nv, ks, vs, all_keys, out):
    keys = (ck[...].astype(F32) * ks[...]).astype(BF16)
    values = (cv[...].astype(F32) * vs[...]).astype(BF16)
    cache = jnp.concatenate([keys, values], axis=1)
    fresh = jnp.concatenate([nk[...], nv[...]], axis=1)
    peak = jnp.max(jnp.abs(all_keys[...].astype(F32)), axis=0, keepdims=True)
    lines = [peak[:, 256 * i : 256 * i + 256] for i in range(4)]
    lines.append(jnp.zeros((12, 256), F32))
    peaks = jnp.concatenate(lines, axis=0).astype(BF16)
    for k in range(NY):
        out[k, :CROWS, :] = cache
        out[k, CROWS:HALF, :] = fresh
        out[k, HALF:, :] = peaks


def pack(place, ck, cv, nk, nv, ks, vs):
    row = lambda i, p: (p[3], p[2])
    top = lambda i, p: (0, p[2])
    return pl.pallas_call(
        pack_kernel,
        out_shape=jax.ShapeDtypeStruct((NY, SENT, 2 * ATT_DIM), BF16),
        grid_spec=pltpu.PrefetchScalarGridSpec(
            num_scalar_prefetch=1,
            grid=(1,),
            in_specs=[
                pl.BlockSpec((CROWS, ATT_DIM), row),
                pl.BlockSpec((CROWS, ATT_DIM), row),
                pl.BlockSpec((NROWS, ATT_DIM), row),
                pl.BlockSpec((NROWS, ATT_DIM), row),
                pl.BlockSpec((1, ATT_DIM), top),
                pl.BlockSpec((1, ATT_DIM), top),
                pl.BlockSpec((TOK, KV_HEADS * ATT_DIM), lambda i, p: (0, 0)),
            ],
            out_specs=pl.BlockSpec((NY, SENT, 2 * ATT_DIM), lambda i, p: (0, 0, 0)),
        ),
        cost_estimate=pl.CostEstimate(flops=1000000, bytes_accessed=1 << 21, transcendentals=0),
        compiler_params=pltpu.CompilerParams(vmem_limit_bytes=58 << 20),
        name="pack",
    )(place, ck, cv, nk, nv, ks, vs, nk)


def local_kernel(place, x, step_t, b_map, rate_of, forget, send, run_out, run_t_out):
    rows = lax.broadcasted_iota(jnp.int32, (TOK, TOK), 0)
    cols = lax.broadcasted_iota(jnp.int32, (TOK, TOK), 1)
    square = lax.broadcasted_iota(jnp.int32, (HEADS, HEADS), 0) == lax.broadcasted_iota(
        jnp.int32, (HEADS, HEADS), 1
    )
    rate_col = jnp.sum(jnp.where(square, rate_of[...], 0.0), axis=1, keepdims=True)
    rate_t = -rate_col * step_t[...] - forget[...]
    run_t = jnp.dot(
        rate_t, (rows <= cols).astype(F32), precision=HIGHEST, preferred_element_type=F32
    )
    run_t_out[...] = run_t
    run_out[...] = run_t.T
    last = run_t[:, TOK - 1 : TOK]
    gain = spread_heads((jnp.exp(last - run_t) * step_t[...]).T)
    given = (x[...].astype(F32) * gain).astype(BF16)
    local = lax.dot_general(
        b_map[...], given, (((0,), (0,)), ((), ())), preferred_element_type=F32
    ).astype(BF16)
    final = jnp.sum(jnp.where(square, last, 0.0), axis=0, keepdims=True)
    decay = spread_heads(jnp.exp(jnp.broadcast_to(final, (8, HEADS))))[0:1, :]
    hi = decay.astype(BF16)
    low = (decay - hi.astype(F32)).astype(BF16)
    for d in range(ND):
        block, half = d // 2, d % 2
        tail = []
        for source in (hi, low):
            for j in range(4):
                at = (half * 4 + j) * 128
                tail.append(source[:, at : at + 128].astype(F32))
        for j in range(4):
            at = (half * 4 + j) * 128
            send[d, 16 * j : 16 * j + 16, :] = local[16 * block : 16 * block + 16, at : at + 128]
        send[d, BACK:, :] = jnp.concatenate(tail, axis=0).astype(BF16)


def within_kernel(place, x, step_t, running, run_t, b_map, c_map, skip, base):
    rows = lax.broadcasted_iota(jnp.int32, (TOK, TOK), 0)
    cols = lax.broadcasted_iota(jnp.int32, (TOK, TOK), 1)
    causal = rows >= cols
    gram = lax.dot_general(
        c_map[...], b_map[...], (((1,), (1,)), ((), ())), preferred_element_type=F32
    )
    signal = x[...].astype(F32)
    given = (signal * spread_heads(step_t[...].T)).astype(BF16)
    skips = spread_heads(jnp.broadcast_to(skip[...], (8, HEADS)))[0:1, :]
    low = lax.broadcasted_iota(jnp.int32, (TOK, 128), 1) < HEAD_DIM
    for j in range(HEADS // 2):
        sides = []
        part = given[:, 128 * j : 128 * j + 128]
        for h in (2 * j, 2 * j + 1):
            spread = running[:, h : h + 1] - run_t[h : h + 1, :]
            weight = jnp.exp(jnp.where(causal, spread, NEG)) * gram
            sides.append(jnp.dot(weight.astype(BF16), part, preferred_element_type=F32))
        at = slice(128 * j, 128 * j + 128)
        base[:, at] = jnp.where(low, sides[0], sides[1]) + skips[:, at] * signal[:, at]


def scan_kernel(place, recv, send):
    states = [jnp.zeros((16, 128), F32) for _ in range(4)]
    for s in range(ND):
        tail = recv[s, BACK:, :].astype(F32)
        for j in range(4):
            send[s, 16 * j : 16 * j + 16, :] = states[j].astype(BF16)
            decay = tail[j : j + 1, :] + tail[4 + j : 5 + j, :]
            states[j] = decay * states[j] + recv[s, 16 * j : 16 * j + 16, :].astype(F32)


def final_kernel(place, recv, base, c_map, running, out, carried):
    for d in range(ND):
        block, half = d // 2, d % 2
        for j in range(4):
            at = (half * 4 + j) * 128
            carried[16 * block : 16 * block + 16, at : at + 128] = recv[d, 16 * j : 16 * j + 16, :]
    prior = jnp.dot(c_map[...], carried[...], preferred_element_type=F32)
    out[...] = (base[...] + spread_heads(jnp.exp(running[...])) * prior).astype(BF16)


CACHED = 2 * NY * CROWS
FRESH = 2 * NY * NROWS
CHUNK = 256


def load_keys(pieces, keys, values):
    at = 0
    for first, count in ((0, CROWS), (CROWS, NROWS)):
        for ref in pieces:
            size = NY * count
            both = ref[:, first : first + count, :].reshape(size, 2 * ATT_DIM)
            keys[at : at + size, :] = both[:, :ATT_DIM]
            values[at : at + size, :ATT_DIM] = both[:, ATT_DIM:]
            at += size
    values[:, ATT_DIM:] = jnp.ones((NY * 2 * HALF, ATT_DIM), BF16)


def positions(place):
    col = lax.broadcasted_iota(jnp.int32, (1, FRESH), 1)
    base = jnp.zeros((1, FRESH), jnp.int32)
    for k in range(2 * NY):
        side = place[3] if k < NY else 1 - place[3]
        start = k % NY * TOK + side * NROWS - k * NROWS
        base = jnp.where(col >= k * NROWS, start, base)
    return col + base


def attend_kernel(own, place, *refs):
    count = 1 if own else NX - 1
    queries, pieces = refs[:count], refs[count : count + 2]
    outs = refs[count + 2 : 2 * count + 2]
    keys, values, q_rows, sums = refs[2 * count + 2 :]
    mine = place[0]
    load_keys(pieces, keys, values)
    for b in range(count):
        for h in range(QH):
            q_rows[b, h * TOK : (h + 1) * TOK, :] = queries[b][:, h * ATT_DIM : (h + 1) * ATT_DIM]

    def attend_block(b, last):
        q = q_rows[b]
        carry = None
        if own:
            pos = positions(place)
            row = lax.broadcasted_iota(jnp.int32, (TOK, 1), 0) + place[1] * TOK
            row = jnp.concatenate([row] * QH, axis=0)
        for at in range(0, last, CHUNK):
            scores = lax.dot_general(
                q, keys[at : at + CHUNK, :], (((1,), (1,)), ((), ())), preferred_element_type=F32
            )
            if own and at >= CACHED:
                seen = pos[:, at - CACHED : at - CACHED + CHUNK] <= row
                scores = jnp.where(seen, scores, NEG)
            best = jnp.max(jnp.maximum(scores[:, :128], scores[:, 128:]), axis=1, keepdims=True)
            top = best if carry is None else jnp.maximum(carry[1], best)
            probs = jnp.exp2(scores * SCALE - top * SCALE).astype(BF16)
            summed = jnp.dot(probs, values[at : at + CHUNK, :], preferred_element_type=F32)
            if carry is not None:
                summed += carry[0] * jnp.exp2((carry[1] - top) * SCALE)
            carry = (summed, top)
        summed, top = carry
        total = summed[:, ATT_DIM:]
        sums[b, :, :ATT_DIM] = summed[:, :ATT_DIM] / total
        sums[b, :, ATT_DIM:] = top * SCALE + jnp.log2(total)

    if own:
        attend_block(0, CACHED + FRESH)
    else:

        @pl.loop(0, count)
        def _(b):
            owner = lax.rem(mine + b + 1, NX)

            @pl.when(owner > mine)
            def _():
                attend_block(b, CACHED + FRESH)

            @pl.when(owner < mine)
            def _():
                attend_block(b, CACHED)

    peaks = jnp.max(pieces[0][:, HALF:, :].astype(F32), axis=0)
    peaks = jnp.concatenate(
        [peaks[r // 2 : r // 2 + 1, r % 2 * 128 : r % 2 * 128 + 128] for r in range(8)], axis=0
    )
    diagonal = lax.broadcasted_iota(jnp.int32, (128, 128), 0) == lax.broadcasted_iota(
        jnp.int32, (128, 128), 1
    )
    for b in range(count):
        outs[b][:ROWS, :] = sums[b, :, :ATT_DIM].astype(BF16)
        lines = []
        for k in range(ROWS // 128):
            part = sums[b, k * 128 : k * 128 + 128, ATT_DIM:]
            lines.append(jnp.sum(jnp.where(diagonal, part, 0.0), axis=0, keepdims=True))
        lines.append(jnp.zeros((2, ATT_DIM), F32))
        packed = [p.astype(F32) for p in parts_of(jnp.concatenate(lines, axis=0))]
        packed.append(peaks)
        outs[b][ROWS:, :] = jnp.concatenate(packed, axis=0).astype(BF16)


def attend(place, queries, pieces, name):
    count = len(queries)
    partial = jax.ShapeDtypeStruct((ROWS + STAT, ATT_DIM), BF16)
    return call(
        functools.partial(attend_kernel, count == 1),
        [partial] * count,
        (place, *queries, *pieces),
        name,
        count * 4 * ROWS * (CACHED + FRESH) * ATT_DIM,
        scratch=(
            pltpu.VMEM((CACHED + FRESH, ATT_DIM), BF16),
            pltpu.VMEM((CACHED + FRESH, 2 * ATT_DIM), BF16),
            pltpu.VMEM((count, ROWS, ATT_DIM), BF16),
            pltpu.VMEM((count, ROWS, 2 * ATT_DIM), F32),
        ),
    )


def merge_kernel(place, *refs):
    parts, nk, out, codes, scale = refs[:NX], *refs[NX:]
    peaks = functools.reduce(jnp.maximum, [ref[ROWS:, :].astype(F32)[24:32] for ref in parts])
    peaks = jnp.concatenate([peaks[r : r + 1, :] for r in range(8)], axis=1)
    key_scale = (peaks + 1e-6) / 127.0
    scale[...] = key_scale
    codes[...] = (nk[...].astype(F32) / key_scale).astype(BF16)
    diagonal = lax.broadcasted_iota(jnp.int32, (128, 128), 0) == lax.broadcasted_iota(
        jnp.int32, (128, 128), 1
    )
    stats = []
    for ref in parts:
        packed = ref[ROWS:, :].astype(F32)
        stats.append(packed[0:8] + packed[8:16] + packed[16:24])
    top = functools.reduce(jnp.maximum, stats)
    shares = [jnp.exp2(s - top) for s in stats]
    total = functools.reduce(jnp.add, shares)
    shares = [s / total for s in shares]
    pieces = []
    for k in range(ROWS // 128):
        summed = jnp.zeros((128, 128), F32)
        for share, ref in zip(shares, parts):
            line = jnp.where(diagonal, share[k : k + 1, :], 0.0)
            column = jnp.sum(line, axis=1, keepdims=True)
            summed += column * ref[k * 128 : k * 128 + 128, :].astype(F32)
        pieces.append(summed)
    result = jnp.concatenate(pieces, axis=0)
    for h in range(QH):
        out[:, h * ATT_DIM : (h + 1) * ATT_DIM] = result[h * TOK : (h + 1) * TOK, :].astype(BF16)


def shift(value, axis, by):
    size = lax.axis_size(axis)
    return lax.ppermute(value, axis, [(i, (i + by) % size) for i in range(size)])


def body(
    ssm_input,
    state_in,
    state_out,
    step_size,
    decay_rate,
    forget,
    skip_gain,
    queries,
    new_keys,
    new_values,
    cache_keys,
    cache_values,
    cache_key_scale,
    cache_value_scale,
):
    head = lax.axis_index("head")
    step_t = step_size.T
    column, core = head // 2, head % 2
    place = jnp.stack(
        [lax.axis_index("seq_0"), lax.axis_index("seq_1"), column, core]
    ).astype(jnp.int32)

    packed = pack(
        place,
        cache_keys,
        cache_values,
        new_keys,
        new_values,
        cache_key_scale.reshape(1, -1),
        cache_value_scale.reshape(1, -1),
    )
    swap = [(i, i ^ 1) for i in range(lax.axis_size("head"))]
    kv_a = lax.all_to_all(packed, "seq_1", 0, 0, tiled=True)
    q_left = shift(queries, "seq_0", 1)
    q_right = shift(queries, "seq_0", -1)
    q_far = shift(queries, "seq_0", 2)

    b_map = lax.dynamic_slice_in_dim(state_in, column * STATE, STATE, 1)
    c_map = lax.dynamic_slice_in_dim(state_out, column * STATE, STATE, 1)
    send, running, run_t = call(
        local_kernel,
        [
            jax.ShapeDtypeStruct((ND, SLOT, 128), BF16),
            jax.ShapeDtypeStruct((TOK, HEADS), F32),
            jax.ShapeDtypeStruct((HEADS, TOK), F32),
        ],
        (
            place,
            ssm_input,
            step_t,
            b_map,
            decay_rate.reshape(1, -1),
            forget.reshape(1, -1),
        ),
        "local",
        2 * TOK * COLS * STATE,
        after=(packed,),
    )
    kv_a = hold(kv_a, (run_t, q_left, q_right, q_far))
    kv_b = lax.ppermute(kv_a, "head", swap)
    pieces = (kv_a, kv_b)
    send = hold(send, (kv_b,))
    recv = lax.all_to_all(send, SEQ, 0, 0, tiled=True)
    base = call(
        within_kernel,
        jax.ShapeDtypeStruct((TOK, COLS), F32),
        (place, ssm_input, step_t, running, run_t, b_map, c_map, skip_gain.reshape(1, -1)),
        "within",
        4 * TOK * COLS * TOK,
    )
    p_right, p_far, p_left = attend(
        place, (q_right, q_far, q_left), pieces, "attend_others"
    )
    (p_own,) = attend(place, (queries,), pieces, "attend_own")
    back = call(
        scan_kernel,
        jax.ShapeDtypeStruct((ND, BACK, 128), BF16),
        (place, recv),
        "scan",
        1000000,
        after=(base, p_right),
    )
    carried = lax.all_to_all(back, SEQ, 0, 0, tiled=True)

    r_left = shift(p_left, "seq_0", -1)
    r_right = shift(p_right, "seq_0", 1)
    r_far = shift(p_far, "seq_0", 2)
    attended, key_codes, key_scale = call(
        merge_kernel,
        [
            jax.ShapeDtypeStruct((TOK, QH * ATT_DIM), BF16),
            jax.ShapeDtypeStruct((TOK, KV_HEADS * ATT_DIM), BF16),
            jax.ShapeDtypeStruct((1, KV_HEADS * ATT_DIM), F32),
        ],
        (place, p_own, r_left, r_right, r_far, new_keys),
        "merge",
        1000000,
    )
    ssm_output = call(
        final_kernel,
        jax.ShapeDtypeStruct((TOK, COLS), BF16),
        (place, carried, base, c_map, running),
        "final",
        2 * TOK * COLS * STATE,
        scratch=(pltpu.VMEM((STATE, COLS), BF16),),
    )
    return (ssm_output, attended, key_codes, key_scale.reshape(-1))


def solution(mesh):
    split = Mesh(mesh.devices.reshape(NX, NY, mesh.shape["head"]), ("seq_0", "seq_1", "head"))
    return jax.shard_map(
        body,
        mesh=split,
        in_specs=(
            P(SEQ, "head"),
            P(SEQ, None),
            P(SEQ, None),
            P(SEQ, "head"),
            P("head"),
            P(SEQ),
            P("head"),
            P(SEQ, "head"),
            P(SEQ, None),
            P(SEQ, None),
            P(SEQ, None),
            P(SEQ, None),
            P(),
            P(),
        ),
        out_specs=(P(SEQ, "head"), P(SEQ, "head"), P(SEQ, None), P()),
        check_vma=False,
    )
```

time: 137 us -> 94.6 us (0.69)
  waiting for transfers between devices: 40.1 us -> 11.9 us
  Pallas kernels: 44.4 us -> 27 us
  starting transfers between devices: 42.9 us -> 46.8 us
  local copies, waits for them, and re-layouts: 7.53 us -> 5.67 us
    pallas_call x8 -> x10, Pallas kernels: 44.4 us -> 27 us  [the longest x7 24.3 us: call(): pl.pallas_call(inner, out_shape=out_shape, in_specs=[pl.BlockSpec(memory_...]
    all_to_all x1, waiting for transfers between devices: 14 us -> 1.28 us  [body(): recv = lax.all_to_all(send, SEQ, 0, 0, tiled=True)]
    all_to_all x1, waiting for transfers between devices: 16.4 us -> 4.6 us  [body(): kv_a = lax.all_to_all(packed, 'seq_1', 0, 0, tiled=True)]
    ppermute x6, waiting for transfers between devices: 9.67 us -> 4.19 us  [shift(): lax.ppermute(value, axis, [(i, (i + by) % size) for i in range(size)])]
    all_to_all x1, starting transfers between devices: 10.5 us -> 5.71 us  [body(): recv = lax.all_to_all(send, SEQ, 0, 0, tiled=True)]
    ppermute x6, starting transfers between devices: 17.4 us -> 20.2 us  [shift(): lax.ppermute(value, axis, [(i, (i + by) % size) for i in range(size)])]
    all_to_all x1, starting transfers between devices: 5.44 us -> 8.08 us  [body(): carried = lax.all_to_all(back, SEQ, 0, 0, tiled=True)]
    ppermute x1, starting transfers between devices: 3.16 us -> 5.09 us  [body(): kv_b = lax.ppermute(kv_a, 'head', swap)]
  transfers between devices with their start and end apart: 10 -> 10, of which waited for: 5 -> 5; matrix products, arithmetic and copies ran while one was open for 1% -> 1% of each run, Pallas kernels for 28% -> 23%
where the time goes in v2:
time: 94.6 us; the launch traced here: 93 us
  starting transfers between devices  46.8 us (49%)
  Pallas kernels  27 us (29%)
  waiting for transfers between devices  11.9 us (13%)
  local copies, waits for them, and re-layouts  5.67 us (6%)
  between operations  0.96 us (1%)
    pallas_call x7, Pallas kernels, call(): pl.pallas_call(inner, out_shape=out_shape, in_specs=[pl.BlockSpec(memory_...  24.3 us
    ppermute x6, starting transfers between devices, shift(): lax.ppermute(value, axis, [(i, (i + by) % size) for i in range(size)])  20.2 us
    all_to_all x1, starting transfers between devices, body(): carried = lax.all_to_all(back, SEQ, 0, 0, tiled=True)  8.08 us
    all_to_all x1, starting transfers between devices, body(): kv_a = lax.all_to_all(packed, 'seq_1', 0, 0, tiled=True)  7.78 us
    all_to_all x1, starting transfers between devices, body(): recv = lax.all_to_all(send, SEQ, 0, 0, tiled=True)  5.71 us
    ppermute x1, starting transfers between devices, body(): kv_b = lax.ppermute(kv_a, 'head', swap)  5.09 us
    unnamed x46, local copies, waits for them, and re-layouts  4.7 us
    all_to_all x1, waiting for transfers between devices, body(): kv_a = lax.all_to_all(packed, 'seq_1', 0, 0, tiled=True)  4.6 us
  transfers between devices with their start and end apart: 10, of which 5 were waited for; matrix products, arithmetic and copies ran while one was open for 1% of the time, Pallas kernels for 23%

profile of v2, /device:TPU:1, one launch (start us, length us, event | category | flops | bytes accessed | tf_op | source)
XLA Modules:
  0.0 93.0 jit_solution(12001412106349893924)
XLA Ops:
  1.3 2.7 %pack.1.refs_6_ = bf16[8,176,256]{2,1,0:T(8,128)(2,1)} custom-call(s32[4]{0:T(128)} %pad_add_fusion.place.refs_0_, bf16[128,1024]{1,0:T(8,128)(2,1)} %ck.1, bf16[128,1024]{1,0:T(8,128)(2,1)} %cv.1, bf16[192,1024]{1,0:T(8,128)(2,1)} %refs_5_.1, bf16[192,1024]{1,0:T(8,128)(2,1)} %nv.1, f32[1,1024]{1,0:T(1,128)} %bitcast.16, f32[1,1024]{1,0:T(1,128)} %bitcast.17, ...), custom_call_target="tpu_custom_call" | custom-call | flops 1000000 | bytes 2097152 | tf_op jit(solution)/shard_map/pack/pallas_call | solution.py:112
  4.0 7.8 %all-to-all-start = ((bf16[8,176,256]{2,1,0:T(8,128)(2,1)}), bf16[8,176,256]{2,1,0:T(8,128)(2,1)S(1)}, u32[]{:S(2)}, u32[]{:S(2)}) async-start(bf16[8,176,256]{2,1,0:T(8,128)(2,1)} %pack.1.refs_6_), calls=%async_computation | async-start | bytes 1441792 | tf_op jit(solution)/shard_map/all_to_all | solution.py:399
  11.8 3.1 %collective-permute-start = (bf16[192,512]{1,0:T(8,128)(2,1)}, bf16[192,512]{1,0:T(8,128)(2,1)S(1)}, u32[]{:S(2)}, u32[]{:S(2)}) collective-permute-start(bf16[192,512]{1,0:T(8,128)(2,1)} %refs_1_.5), channel_id=1, source_target_pairs={{0,128},{128,256},{256,384},{384,0},{1,129},{129,257},{257,385},{3... | collective-permute-start | bytes 589832 | tf_op jit(solution)/shard_map/ppermute | solution.py:363
  14.9 3.4 %collective-permute-start.1 = (bf16[192,512]{1,0:T(8,128)(2,1)}, bf16[192,512]{1,0:T(8,128)(2,1)S(1)}, u32[]{:S(2)}, u32[]{:S(2)}) collective-permute-start(bf16[192,512]{1,0:T(8,128)(2,1)} %refs_1_.5), channel_id=1, source_target_pairs={{0,384},{128,0},{256,128},{384,256},{1,385},{129,1},{257,129},{385... | collective-permute-start | bytes 589832 | tf_op jit(solution)/shard_map/ppermute | solution.py:363
  18.3 3.4 %collective-permute-start.2 = (bf16[192,512]{1,0:T(8,128)(2,1)}, bf16[192,512]{1,0:T(8,128)(2,1)S(1)}, u32[]{:S(2)}, u32[]{:S(2)}) collective-permute-start(bf16[192,512]{1,0:T(8,128)(2,1)} %refs_1_.5), channel_id=1, source_target_pairs={{0,256},{128,384},{256,0},{384,128},{1,257},{129,385},{257,1},{385... | collective-permute-start | bytes 589832 | tf_op jit(solution)/shard_map/ppermute | solution.py:363
  22.5 2.7 %local.1 = (bf16[32,72,128]{2,1,0:T(8,128)(2,1)}, f32[192,16]{1,0:T(8,128)S(1)}, f32[16,192]{1,0:T(8,128)S(1)}) custom-call(s32[4]{0:T(128)S(1)} %copy-done.17, bf16[192,1024]{1,0:T(8,128)(2,1)S(1)} %copy-done.3, f32[16,192]{1,0:T(8,128)S(1)} %bitcast.11, bf16[192,256]{1,0:T(8,128)(2,1)S(1)} %constant_dynamic-slice_fusion.1.refs_3_.refs_5_, ...), custom_call_target="tpu_custom_call" | custom-call | flops 100663296 | bytes 2097152 | tf_op jit(solution)/shard_map/local/pallas_call | solution.py:50
  25.2 1.5 %collective-permute-done.2.refs_4_.refs_2_ = bf16[192,512]{1,0:T(8,128)(2,1)S(1)} collective-permute-done((bf16[192,512]{1,0:T(8,128)(2,1)}, bf16[192,512]{1,0:T(8,128)(2,1)S(1)}, u32[]{:S(2)}, u32[]{:S(2)}) %collective-permute-start.2) | collective-permute-done | bytes 196640 | tf_op jit(solution)/shard_map/ppermute | solution.py:363
  26.7 4.6 %all-to-all-done.refs_0_ = bf16[8,176,256]{2,1,0:T(8,128)(2,1)S(1)} async-done(((bf16[8,176,256]{2,1,0:T(8,128)(2,1)}), bf16[8,176,256]{2,1,0:T(8,128)(2,1)S(1)}, u32[]{:S(2)}, u32[]{:S(2)}) %all-to-all-start) | async-done | bytes 720928 | tf_op jit(solution)/shard_map/all_to_all | solution.py:399
  31.3 5.1 %collective-permute-start.3 = (bf16[8,176,256]{2,1,0:T(8,128)(2,1)S(1)}, bf16[8,176,256]{2,1,0:T(8,128)(2,1)S(1)}, u32[]{:S(2)}, u32[]{:S(2)}) collective-permute-start(bf16[8,176,256]{2,1,0:T(8,128)(2,1)S(1)} %hold.2.refs_4_.refs_2_), channel_id=1, source_target_pairs={{0,1},{1,0},{2,3},{3,2},{4,5},{5,4},{6,7},{7,6},{8,9},{9,8},{10,11... | collective-permute-start | bytes 2162696 | tf_op jit(solution)/shard_map/ppermute | solution.py:426
  36.4 1.8 %collective-permute-done.3.refs_1_.refs_5_.refs_3_ = bf16[8,176,256]{2,1,0:T(8,128)(2,1)S(1)} collective-permute-done((bf16[8,176,256]{2,1,0:T(8,128)(2,1)S(1)}, bf16[8,176,256]{2,1,0:T(8,128)(2,1)S(1)}, u32[]{:S(2)}, u32[]{:S(2)}) %collective-permute-start.3) | collective-permute-done | bytes 720928 | tf_op jit(solution)/shard_map/ppermute | solution.py:426
  39.1 5.7 %all-to-all-start.1 = ((bf16[32,72,128]{2,1,0:T(8,128)(2,1)}), bf16[32,72,128]{2,1,0:T(8,128)(2,1)S(1)}, u32[]{:S(2)}, u32[]{:S(2)}) async-start(bf16[32,72,128]{2,1,0:T(8,128)(2,1)} %hold.3), calls=%async_computation.1 | async-start | bytes 1179648 | tf_op jit(solution)/shard_map/all_to_all | solution.py:429
  46.4 1.9 %within.1.refs_2_ = f32[192,1024]{1,0:T(8,128)S(1)} custom-call(s32[4]{0:T(128)S(1)} %copy-done.17, bf16[192,1024]{1,0:T(8,128)(2,1)S(1)} %copy-done.3, f32[16,192]{1,0:T(8,128)S(1)} %bitcast.12, f32[192,16]{1,0:T(8,128)S(1)} %copy-done.8, f32[16,192]{1,0:T(8,128)S(1)} %get-tuple-element.14.refs_1_.refs_4_, ...), custom_call_target="tpu_custom_call" | custom-call | flops 150994944 | bytes 2097152 | tf_op jit(solution)/shard_map/within/pallas_call | solution.py:50
  48.4 9.3 %attend_others.1 = (bf16[800,128]{1,0:T(8,128)(2,1)S(1)}, bf16[800,128]{1,0:T(8,128)(2,1)S(1)}, bf16[800,128]{1,0:T(8,128)(2,1)S(1)}) custom-call(s32[4]{0:T(128)S(1)} %copy-done.17, bf16[192,512]{1,0:T(8,128)(2,1)S(1)} %copy-done.13, bf16[192,512]{1,0:T(8,128)(2,1)S(1)} %copy-done.15, bf16[192,512]{1,0:T(8,128)(2,1)S(1)} %copy-done.11, ...), custom_call_target="tpu_custom_call" | custom-call | flops 3019898880 | bytes 2097152 | tf_op jit(solution)/shard_map/attend_others/pallas_call | solution.py:50
  59.1 1.3 %all-to-all-done.1.refs_1_ = bf16[32,72,128]{2,1,0:T(8,128)(2,1)S(1)} async-done(((bf16[32,72,128]{2,1,0:T(8,128)(2,1)}), bf16[32,72,128]{2,1,0:T(8,128)(2,1)S(1)}, u32[]{:S(2)}, u32[]{:S(2)}) %all-to-all-start.1) | async-done | bytes 589856 | tf_op jit(solution)/shard_map/all_to_all | solution.py:429
  60.4 1.5 %scan.1 = bf16[32,64,128]{2,1,0:T(8,128)(2,1)} custom-call(s32[4]{0:T(128)S(1)} %copy-done.17, bf16[32,72,128]{2,1,0:T(8,128)(2,1)S(1)} %all-to-all-done.1.refs_1_, f32[192,1024]{1,0:T(8,128)S(1)} %within.1.refs_2_, bf16[800,128]{1,0:T(8,128)(2,1)S(1)} %get-tuple-element.16.refs_3_), custom_call_target="tpu_custom_call" | custom-call | flops 1000000 | bytes 2097152 | tf_op jit(solution)/shard_map/scan/pallas_call | solution.py:50
  61.9 8.1 %all-to-all-start.2 = ((bf16[32,64,128]{2,1,0:T(8,128)(2,1)}), bf16[32,64,128]{2,1,0:T(8,128)(2,1)S(1)}, u32[]{:S(2)}, u32[]{:S(2)}) async-start(bf16[32,64,128]{2,1,0:T(8,128)(2,1)} %scan.1), calls=%async_computation.2 | async-start | bytes 1048576 | tf_op jit(solution)/shard_map/all_to_all | solution.py:449
  70.0 3.1 %collective-permute-start.5 = (bf16[800,128]{1,0:T(8,128)(2,1)S(1)}, bf16[800,128]{1,0:T(8,128)(2,1)S(1)}, u32[]{:S(2)}, u32[]{:S(2)}) collective-permute-start(bf16[800,128]{1,0:T(8,128)(2,1)S(1)} %get-tuple-element.16.refs_3_), channel_id=1, source_target_pairs={{0,128},{128,256},{256,384},{384,0},{1,129},{129,257},{257,385},{3... | collective-permute-start | bytes 614408 | tf_op jit(solution)/shard_map/ppermute | solution.py:363
  73.1 3.4 %collective-permute-start.4 = (bf16[800,128]{1,0:T(8,128)(2,1)}, bf16[800,128]{1,0:T(8,128)(2,1)S(1)}, u32[]{:S(2)}, u32[]{:S(2)}) collective-permute-start(bf16[800,128]{1,0:T(8,128)(2,1)} %copy-done.22), channel_id=1, source_target_pairs={{0,384},{128,0},{256,128},{384,256},{1,385},{129,1},{257,129},{385... | collective-permute-start | bytes 614408 | tf_op jit(solution)/shard_map/ppermute | solution.py:363
  76.5 3.8 %collective-permute-start.6 = (bf16[800,128]{1,0:T(8,128)(2,1)}, bf16[800,128]{1,0:T(8,128)(2,1)S(1)}, u32[]{:S(2)}, u32[]{:S(2)}) collective-permute-start(bf16[800,128]{1,0:T(8,128)(2,1)} %copy-done.21), channel_id=1, source_target_pairs={{0,256},{128,384},{256,0},{384,128},{1,257},{129,385},{257,1},{385... | collective-permute-start | bytes 614408 | tf_op jit(solution)/shard_map/ppermute | solution.py:363
  80.3 1.1 %copy-done.6 = bf16[8,176,256]{2,1,0:T(8,128)(2,1)S(1)} copy-done((bf16[8,176,256]{2,1,0:T(8,128)(2,1)S(1)}, bf16[8,176,256]{2,1,0:T(8,128)(2,1)}, u32[]{:S(2)}) %copy-start.6) | copy-done | bytes 720920
  81.4 5.1 %attend_own.1.refs_1_ = bf16[800,128]{1,0:T(8,128)(2,1)S(1)} custom-call(s32[4]{0:T(128)S(1)} %copy-done.17, bf16[192,512]{1,0:T(8,128)(2,1)} %refs_1_.5, bf16[8,176,256]{2,1,0:T(8,128)(2,1)S(1)} %hold.2.refs_4_.refs_2_, bf16[8,176,256]{2,1,0:T(8,128)(2,1)S(1)} %copy-done.6), custom_call_target="tpu_custom_call" | custom-call | flops 1006632960 | bytes 2097152 | tf_op jit(solution)/shard_map/attend_own/pallas_call | solution.py:50
  86.5 2.7 %collective-permute-done.6.refs_4_ = bf16[800,128]{1,0:T(8,128)(2,1)S(1)} collective-permute-done((bf16[800,128]{1,0:T(8,128)(2,1)}, bf16[800,128]{1,0:T(8,128)(2,1)S(1)}, u32[]{:S(2)}, u32[]{:S(2)}) %collective-permute-start.6) | collective-permute-done | bytes 204832 | tf_op jit(solution)/shard_map/ppermute | solution.py:363
  89.2 1.9 %merge.1 = (bf16[192,512]{1,0:T(8,128)(2,1)}, bf16[192,1024]{1,0:T(8,128)(2,1)}, f32[1,1024]{1,0:T(1,128)}) custom-call(s32[4]{0:T(128)S(1)} %copy-done.17, bf16[800,128]{1,0:T(8,128)(2,1)S(1)} %attend_own.1.refs_1_, bf16[800,128]{1,0:T(8,128)(2,1)S(1)} %collective-permute-done.4.refs_2_, bf16[800,128]{1,0:T(8,128)(2,1)S(1)} %collective-permute-done.5.refs_3_, ...), custom_call_target="tpu_custom_call" | custom-call | flops 1000000 | bytes 2097152 | tf_op jit(solution)/shard_map/merge/pallas_call | solution.py:50
  91.1 1.9 %final.1 = bf16[192,1024]{1,0:T(8,128)(2,1)} custom-call(s32[4]{0:T(128)S(1)} %copy-done.17, bf16[32,64,128]{2,1,0:T(8,128)(2,1)S(1)} %all-to-all-done.2.refs_1_, f32[192,1024]{1,0:T(8,128)S(1)} %within.1.refs_2_, bf16[192,256]{1,0:T(8,128)(2,1)S(1)} %constant_dynamic-slice_fusion.refs_6_.refs_3_, f32[192,16]{1,0:T(8,128)S(1)} %copy-done.9), custom_call_target="tpu_custom_call" | custom-call | flops 100663296 | bytes 2097152 | tf_op jit(solution)/shard_map/final/pallas_call | solution.py:50
  (55 shorter events, 5.2 us)
Async XLA Ops:
  0.6 21.1 %copy-start = (bf16[192,2048]{1,0:T(8,128)(2,1)S(1)}, bf16[192,2048]{1,0:T(8,128)(2,1)}, u32[]{:S(2)}) copy-start(bf16[192,2048]{1,0:T(8,128)(2,1)} %param.15) | copy-start | bytes 2359300
  4.0 17.8 %copy-start.1 = (bf16[8,176,256]{2,1,0:T(8,128)(2,1)S(1)}, bf16[8,176,256]{2,1,0:T(8,128)(2,1)}, u32[]{:S(2)}) copy-start(bf16[8,176,256]{2,1,0:T(8,128)(2,1)} %pack.1.refs_6_) | copy-start | bytes 2162692
  4.0 17.8 %copy-start.3 = (bf16[192,1024]{1,0:T(8,128)(2,1)S(1)}, bf16[192,1024]{1,0:T(8,128)(2,1)}, u32[]{:S(2)}) copy-start(bf16[192,1024]{1,0:T(8,128)(2,1)} %refs_1_.4) | copy-start | bytes 1179652
  4.0 27.3 %all-to-all-start = ((bf16[8,176,256]{2,1,0:T(8,128)(2,1)}), bf16[8,176,256]{2,1,0:T(8,128)(2,1)S(1)}, u32[]{:S(2)}, u32[]{:S(2)}) async-start(bf16[8,176,256]{2,1,0:T(8,128)(2,1)} %pack.1.refs_6_), calls=%async_computation | async-start | bytes 1441792 | tf_op jit(solution)/shard_map/all_to_all | solution.py:399
  11.8 13.4 %collective-permute-start = (bf16[192,512]{1,0:T(8,128)(2,1)}, bf16[192,512]{1,0:T(8,128)(2,1)S(1)}, u32[]{:S(2)}, u32[]{:S(2)}) collective-permute-start(bf16[192,512]{1,0:T(8,128)(2,1)} %refs_1_.5), channel_id=1, source_target_pairs={{0,128},{128,256},{256,384},{384,0},{1,129},{129,257},{257,385},{3... | collective-permute-start | bytes 589832 | tf_op jit(solution)/shard_map/ppermute | solution.py:363
  14.9 10.3 %collective-permute-start.1 = (bf16[192,512]{1,0:T(8,128)(2,1)}, bf16[192,512]{1,0:T(8,128)(2,1)S(1)}, u32[]{:S(2)}, u32[]{:S(2)}) collective-permute-start(bf16[192,512]{1,0:T(8,128)(2,1)} %refs_1_.5), channel_id=1, source_target_pairs={{0,384},{128,0},{256,128},{384,256},{1,385},{129,1},{257,129},{385... | collective-permute-start | bytes 589832 | tf_op jit(solution)/shard_map/ppermute | solution.py:363
  18.3 8.4 %collective-permute-start.2 = (bf16[192,512]{1,0:T(8,128)(2,1)}, bf16[192,512]{1,0:T(8,128)(2,1)S(1)}, u32[]{:S(2)}, u32[]{:S(2)}) collective-permute-start(bf16[192,512]{1,0:T(8,128)(2,1)} %refs_1_.5), channel_id=1, source_target_pairs={{0,256},{128,384},{256,0},{384,128},{1,257},{129,385},{257,1},{385... | collective-permute-start | bytes 589832 | tf_op jit(solution)/shard_map/ppermute | solution.py:363
  25.2 6.1 %copy-start.7 = (f32[192,16]{1,0:T(8,128)}, f32[192,16]{1,0:T(8,128)S(1)}, u32[]{:S(2)}) copy-start(f32[192,16]{1,0:T(8,128)S(1)} %get-tuple-element.15.refs_3_.refs_4_) | copy-start | bytes 36868
  25.2 6.1 %copy-start.10 = (bf16[192,512]{1,0:T(8,128)(2,1)}, bf16[192,512]{1,0:T(8,128)(2,1)S(1)}, u32[]{:S(2)}) copy-start(bf16[192,512]{1,0:T(8,128)(2,1)S(1)} %collective-permute-done.refs_2_.refs_3_) | copy-start | bytes 589828
  25.2 6.1 %copy-start.12 = (bf16[192,512]{1,0:T(8,128)(2,1)}, bf16[192,512]{1,0:T(8,128)(2,1)S(1)}, u32[]{:S(2)}) copy-start(bf16[192,512]{1,0:T(8,128)(2,1)S(1)} %collective-permute-done.1.refs_3_.refs_1_) | copy-start | bytes 589828
  26.7 4.6 %copy-start.14 = (bf16[192,512]{1,0:T(8,128)(2,1)}, bf16[192,512]{1,0:T(8,128)(2,1)S(1)}, u32[]{:S(2)}) copy-start(bf16[192,512]{1,0:T(8,128)(2,1)S(1)} %collective-permute-done.2.refs_4_.refs_2_) | copy-start | bytes 589828
  31.3 6.9 %collective-permute-start.3 = (bf16[8,176,256]{2,1,0:T(8,128)(2,1)S(1)}, bf16[8,176,256]{2,1,0:T(8,128)(2,1)S(1)}, u32[]{:S(2)}, u32[]{:S(2)}) collective-permute-start(bf16[8,176,256]{2,1,0:T(8,128)(2,1)S(1)} %hold.2.refs_4_.refs_2_), channel_id=1, source_target_pairs={{0,1},{1,0},{2,3},{3,2},{4,5},{5,4},{6,7},{7,6},{8,9},{9,8},{10,11... | collective-permute-start | bytes 2162696 | tf_op jit(solution)/shard_map/ppermute | solution.py:426
  39.1 21.3 %all-to-all-start.1 = ((bf16[32,72,128]{2,1,0:T(8,128)(2,1)}), bf16[32,72,128]{2,1,0:T(8,128)(2,1)S(1)}, u32[]{:S(2)}, u32[]{:S(2)}) async-start(bf16[32,72,128]{2,1,0:T(8,128)(2,1)} %hold.3), calls=%async_computation.1 | async-start | bytes 1179648 | tf_op jit(solution)/shard_map/all_to_all | solution.py:429
  46.4 2.0 %copy-start.5 = (bf16[8,176,256]{2,1,0:T(8,128)(2,1)S(1)}, bf16[8,176,256]{2,1,0:T(8,128)(2,1)}, u32[]{:S(2)}) copy-start(bf16[8,176,256]{2,1,0:T(8,128)(2,1)} %copy-done.4) | copy-start | bytes 2162692
  46.4 2.0 %copy-start.11 = (bf16[192,512]{1,0:T(8,128)(2,1)S(1)}, bf16[192,512]{1,0:T(8,128)(2,1)}, u32[]{:S(2)}) copy-start(bf16[192,512]{1,0:T(8,128)(2,1)} %copy-done.10) | copy-start | bytes 589828
  46.4 2.0 %copy-start.13 = (bf16[192,512]{1,0:T(8,128)(2,1)S(1)}, bf16[192,512]{1,0:T(8,128)(2,1)}, u32[]{:S(2)}) copy-start(bf16[192,512]{1,0:T(8,128)(2,1)} %copy-done.12) | copy-start | bytes 589828
  46.4 2.0 %copy-start.15 = (bf16[192,512]{1,0:T(8,128)(2,1)S(1)}, bf16[192,512]{1,0:T(8,128)(2,1)}, u32[]{:S(2)}) copy-start(bf16[192,512]{1,0:T(8,128)(2,1)} %copy-done.14) | copy-start | bytes 589828
  61.9 29.2 %all-to-all-start.2 = ((bf16[32,64,128]{2,1,0:T(8,128)(2,1)}), bf16[32,64,128]{2,1,0:T(8,128)(2,1)S(1)}, u32[]{:S(2)}, u32[]{:S(2)}) async-start(bf16[32,64,128]{2,1,0:T(8,128)(2,1)} %scan.1), calls=%async_computation.2 | async-start | bytes 1048576 | tf_op jit(solution)/shard_map/all_to_all | solution.py:449
  70.0 16.5 %collective-permute-start.5 = (bf16[800,128]{1,0:T(8,128)(2,1)S(1)}, bf16[800,128]{1,0:T(8,128)(2,1)S(1)}, u32[]{:S(2)}, u32[]{:S(2)}) collective-permute-start(bf16[800,128]{1,0:T(8,128)(2,1)S(1)} %get-tuple-element.16.refs_3_), channel_id=1, source_target_pairs={{0,128},{128,256},{256,384},{384,0},{1,129},{129,257},{257,385},{3... | collective-permute-start | bytes 614408 | tf_op jit(solution)/shard_map/ppermute | solution.py:363
  73.1 13.3 %collective-permute-start.4 = (bf16[800,128]{1,0:T(8,128)(2,1)}, bf16[800,128]{1,0:T(8,128)(2,1)S(1)}, u32[]{:S(2)}, u32[]{:S(2)}) collective-permute-start(bf16[800,128]{1,0:T(8,128)(2,1)} %copy-done.22), channel_id=1, source_target_pairs={{0,384},{128,0},{256,128},{384,256},{1,385},{129,1},{257,129},{385... | collective-permute-start | bytes 614408 | tf_op jit(solution)/shard_map/ppermute | solution.py:363
  76.5 12.7 %copy-start.2 = (bf16[192,1024]{1,0:T(8,128)(2,1)S(1)}, bf16[192,1024]{1,0:T(8,128)(2,1)}, u32[]{:S(2)}) copy-start(bf16[192,1024]{1,0:T(8,128)(2,1)} %refs_5_.1) | copy-start | bytes 1179652
  76.5 12.7 %collective-permute-start.6 = (bf16[800,128]{1,0:T(8,128)(2,1)}, bf16[800,128]{1,0:T(8,128)(2,1)S(1)}, u32[]{:S(2)}, u32[]{:S(2)}) collective-permute-start(bf16[800,128]{1,0:T(8,128)(2,1)} %copy-done.21), channel_id=1, source_target_pairs={{0,256},{128,384},{256,0},{384,128},{1,257},{129,385},{257,1},{385... | collective-permute-start | bytes 614408 | tf_op jit(solution)/shard_map/ppermute | solution.py:363
  80.2 1.1 %copy-start.6 = (bf16[8,176,256]{2,1,0:T(8,128)(2,1)S(1)}, bf16[8,176,256]{2,1,0:T(8,128)(2,1)}, u32[]{:S(2)}) copy-start(bf16[8,176,256]{2,1,0:T(8,128)(2,1)} %copy-done.4) | copy-start | bytes 2162692
  86.4 4.7 %copy-start.9 = (f32[192,16]{1,0:T(8,128)S(1)}, f32[192,16]{1,0:T(8,128)}, u32[]{:S(2)}) copy-start(f32[192,16]{1,0:T(8,128)} %copy-done.7) | copy-start | bytes 36868
  (9 other events, 6.6 us)

commit v3 on v2

--- a/solution.py
+++ b/solution.py
@@ -317,7 +317,7 @@
         [partial] * count,
         (place, *queries, *pieces),
         name,
-        count * 4 * ROWS * (CACHED + FRESH) * ATT_DIM,
+        60_000_000_000 if count > 1 else 4 * ROWS * (CACHED + FRESH) * ATT_DIM,
         scratch=(
             pltpu.VMEM((CACHED + FRESH, ATT_DIM), BF16),
             pltpu.VMEM((CACHED + FRESH, 2 * ATT_DIM), BF16),
@@ -425,26 +425,27 @@
     kv_a = hold(kv_a, (run_t, q_left, q_right, q_far))
     kv_b = lax.ppermute(kv_a, "head", swap)
     pieces = (kv_a, kv_b)
-    send = hold(send, (kv_b,))
+    send = hold(send, (kv_a,))
     recv = lax.all_to_all(send, SEQ, 0, 0, tiled=True)
+    p_right, p_far, p_left = attend(
+        place, (q_right, q_far, q_left), pieces, "attend_others"
+    )
+    (p_own,) = attend(place, (queries,), pieces, "attend_own")
     base = call(
         within_kernel,
         jax.ShapeDtypeStruct((TOK, COLS), F32),
         (place, ssm_input, step_t, running, run_t, b_map, c_map, skip_gain.reshape(1, -1)),
         "within",
         4 * TOK * COLS * TOK,
-    )
-    p_right, p_far, p_left = attend(
-        place, (q_right, q_far, q_left), pieces, "attend_others"
-    )
-    (p_own,) = attend(place, (queries,), pieces, "attend_own")
+        after=(p_right,),
+    )
     back = call(
         scan_kernel,
         jax.ShapeDtypeStruct((ND, BACK, 128), BF16),
         (place, recv),
         "scan",
         1000000,
-        after=(base, p_right),
+        after=(base, p_left),
     )
     carried = lax.all_to_all(back, SEQ, 0, 0, tiled=True)
 

time: 94.6 us -> 92.8 us (0.981)
  waiting for transfers between devices: 11.9 us -> 8.09 us
  local copies, waits for them, and re-layouts: 5.67 us -> 9.2 us
    unnamed x46 -> x50, local copies, waits for them, and re-layouts: 4.7 us -> 8.27 us
    ppermute x1, waiting for transfers between devices: 1.8 us -> 0.01 us  [body(): kv_b = lax.ppermute(kv_a, 'head', swap)]
    all_to_all x1, waiting for transfers between devices: 1.28 us -> 0.01 us  [body(): recv = lax.all_to_all(send, SEQ, 0, 0, tiled=True)]
    ppermute x6, starting transfers between devices: 20.2 us -> 21.4 us  [shift(): lax.ppermute(value, axis, [(i, (i + by) % size) for i in range(size)])]
    all_to_all x1, waiting for transfers between devices: 4.6 us -> 3.4 us  [body(): kv_a = lax.all_to_all(packed, 'seq_1', 0, 0, tiled=True)]
    all_to_all x1, starting transfers between devices: 8.08 us -> 6.94 us  [body(): carried = lax.all_to_all(back, SEQ, 0, 0, tiled=True)]
  transfers between devices with their start and end apart: 10 -> 10, of which waited for: 5 -> 3; matrix products, arithmetic and copies ran while one was open for 1% -> 1% of each run, Pallas kernels for 23% -> 23%
where the time goes in v3:
time: 92.8 us; the launch traced here: 91.9 us
  starting transfers between devices  46 us (50%)
  Pallas kernels  27 us (29%)
  local copies, waits for them, and re-layouts  9.2 us (10%)
  waiting for transfers between devices  8.09 us (9%)
  between operations  0.95 us (1%)
    pallas_call x7, Pallas kernels, call(): pl.pallas_call(inner, out_shape=out_shape, in_specs=[pl.BlockSpec(memory_...  24.3 us
    ppermute x6, starting transfers between devices, shift(): lax.ppermute(value, axis, [(i, (i + by) % size) for i in range(size)])  21.4 us
    unnamed x50, local copies, waits for them, and re-layouts  8.27 us
    all_to_all x1, starting transfers between devices, body(): kv_a = lax.all_to_all(packed, 'seq_1', 0, 0, tiled=True)  7.78 us
    all_to_all x1, starting transfers between devices, body(): carried = lax.all_to_all(back, SEQ, 0, 0, tiled=True)  6.94 us
    ppermute x1, starting transfers between devices, body(): kv_b = lax.ppermute(kv_a, 'head', swap)  5.09 us
    all_to_all x1, starting transfers between devices, body(): recv = lax.all_to_all(send, SEQ, 0, 0, tiled=True)  4.81 us
    ppermute x6, waiting for transfers between devices, shift(): lax.ppermute(value, axis, [(i, (i + by) % size) for i in range(size)])  4.68 us
  transfers between devices with their start and end apart: 10, of which 3 were waited for; matrix products, arithmetic and copies ran while one was open for 1% of the time, Pallas kernels for 23%

profile of v3, /device:TPU:1, one launch (start us, length us, event | category | flops | bytes accessed | tf_op | source)
XLA Modules:
  0.0 91.9 jit_solution(15870692796646089223)
XLA Ops:
  1.3 2.8 %pack.1.refs_6_ = bf16[8,176,256]{2,1,0:T(8,128)(2,1)} custom-call(s32[4]{0:T(128)} %pad_add_fusion.place.refs_0_, bf16[128,1024]{1,0:T(8,128)(2,1)} %ck.1, bf16[128,1024]{1,0:T(8,128)(2,1)} %cv.1, bf16[192,1024]{1,0:T(8,128)(2,1)} %refs_5_.1, bf16[192,1024]{1,0:T(8,128)(2,1)} %nv.1, f32[1,1024]{1,0:T(1,128)} %bitcast.16, f32[1,1024]{1,0:T(1,128)} %bitcast.17, ...), custom_call_target="tpu_custom_call" | custom-call | flops 1000000 | bytes 2097152 | tf_op jit(solution)/shard_map/pack/pallas_call | solution.py:112
  4.1 7.8 %all-to-all-start = ((bf16[8,176,256]{2,1,0:T(8,128)(2,1)}), bf16[8,176,256]{2,1,0:T(8,128)(2,1)S(1)}, u32[]{:S(2)}, u32[]{:S(2)}) async-start(bf16[8,176,256]{2,1,0:T(8,128)(2,1)} %pack.1.refs_6_), calls=%async_computation | async-start | bytes 1441792 | tf_op jit(solution)/shard_map/all_to_all | solution.py:399
  11.9 4.4 %collective-permute-start.1 = (bf16[192,512]{1,0:T(8,128)(2,1)}, bf16[192,512]{1,0:T(8,128)(2,1)S(1)}, u32[]{:S(2)}, u32[]{:S(2)}) collective-permute-start(bf16[192,512]{1,0:T(8,128)(2,1)} %refs_1_.5), channel_id=1, source_target_pairs={{0,384},{128,0},{256,128},{384,256},{1,385},{129,1},{257,129},{385... | collective-permute-start | bytes 589832 | tf_op jit(solution)/shard_map/ppermute | solution.py:363
  16.3 1.9 %collective-permute-start = (bf16[192,512]{1,0:T(8,128)(2,1)}, bf16[192,512]{1,0:T(8,128)(2,1)S(1)}, u32[]{:S(2)}, u32[]{:S(2)}) collective-permute-start(bf16[192,512]{1,0:T(8,128)(2,1)} %refs_1_.5), channel_id=1, source_target_pairs={{0,128},{128,256},{256,384},{384,0},{1,129},{129,257},{257,385},{3... | collective-permute-start | bytes 589832 | tf_op jit(solution)/shard_map/ppermute | solution.py:363
  18.2 3.6 %collective-permute-start.2 = (bf16[192,512]{1,0:T(8,128)(2,1)}, bf16[192,512]{1,0:T(8,128)(2,1)S(1)}, u32[]{:S(2)}, u32[]{:S(2)}) collective-permute-start(bf16[192,512]{1,0:T(8,128)(2,1)} %refs_1_.5), channel_id=1, source_target_pairs={{0,256},{128,384},{256,0},{384,128},{1,257},{129,385},{257,1},{385... | collective-permute-start | bytes 589832 | tf_op jit(solution)/shard_map/ppermute | solution.py:363
  22.6 2.7 %local.1 = (bf16[32,72,128]{2,1,0:T(8,128)(2,1)}, f32[192,16]{1,0:T(8,128)S(1)}, f32[16,192]{1,0:T(8,128)S(1)}) custom-call(s32[4]{0:T(128)S(1)} %copy-done.18, bf16[192,1024]{1,0:T(8,128)(2,1)S(1)} %copy-done.3, f32[16,192]{1,0:T(8,128)S(1)} %bitcast.11, bf16[192,256]{1,0:T(8,128)(2,1)S(1)} %constant_dynamic-slice_fusion.1.refs_3_.refs_5_, ...), custom_call_target="tpu_custom_call" | custom-call | flops 100663296 | bytes 2097152 | tf_op jit(solution)/shard_map/local/pallas_call | solution.py:50
  25.3 2.7 %collective-permute-done.2.refs_4_.refs_2_ = bf16[192,512]{1,0:T(8,128)(2,1)S(1)} collective-permute-done((bf16[192,512]{1,0:T(8,128)(2,1)}, bf16[192,512]{1,0:T(8,128)(2,1)S(1)}, u32[]{:S(2)}, u32[]{:S(2)}) %collective-permute-start.2) | collective-permute-done | bytes 196640 | tf_op jit(solution)/shard_map/ppermute | solution.py:363
  28.0 3.4 %all-to-all-done.refs_0_ = bf16[8,176,256]{2,1,0:T(8,128)(2,1)S(1)} async-done(((bf16[8,176,256]{2,1,0:T(8,128)(2,1)}), bf16[8,176,256]{2,1,0:T(8,128)(2,1)S(1)}, u32[]{:S(2)}, u32[]{:S(2)}) %all-to-all-start) | async-done | bytes 720928 | tf_op jit(solution)/shard_map/all_to_all | solution.py:399
  31.4 5.1 %collective-permute-start.3 = (bf16[8,176,256]{2,1,0:T(8,128)(2,1)S(1)}, bf16[8,176,256]{2,1,0:T(8,128)(2,1)S(1)}, u32[]{:S(2)}, u32[]{:S(2)}) collective-permute-start(bf16[8,176,256]{2,1,0:T(8,128)(2,1)S(1)} %hold.2.refs_1_.refs_4_.refs_2_), channel_id=1, source_target_pairs={{0,1},{1,0},{2,3},{3,2},{4,5},{5,4},{6,7},{7,6},{8,9},{9,8},{10,11... | collective-permute-start | bytes 2162696 | tf_op jit(solution)/shard_map/ppermute | solution.py:426
  37.4 4.8 %all-to-all-start.1 = ((bf16[32,72,128]{2,1,0:T(8,128)(2,1)}), bf16[32,72,128]{2,1,0:T(8,128)(2,1)S(1)}, u32[]{:S(2)}, u32[]{:S(2)}) async-start(bf16[32,72,128]{2,1,0:T(8,128)(2,1)} %hold.3), calls=%async_computation.1 | async-start | bytes 1179648 | tf_op jit(solution)/shard_map/all_to_all | solution.py:429
  42.3 0.9 %copy-done.12 = bf16[192,512]{1,0:T(8,128)(2,1)S(1)} copy-done((bf16[192,512]{1,0:T(8,128)(2,1)S(1)}, bf16[192,512]{1,0:T(8,128)(2,1)}, u32[]{:S(2)}) %copy-start.12) | copy-done | bytes 196632
  45.1 9.3 %attend_others.1 = (bf16[800,128]{1,0:T(8,128)(2,1)S(1)}, bf16[800,128]{1,0:T(8,128)(2,1)S(1)}, bf16[800,128]{1,0:T(8,128)(2,1)S(1)}) custom-call(s32[4]{0:T(128)S(1)} %copy-done.18, bf16[192,512]{1,0:T(8,128)(2,1)S(1)} %copy-done.12, bf16[192,512]{1,0:T(8,128)(2,1)S(1)} %copy-done.16, bf16[192,512]{1,0:T(8,128)(2,1)S(1)} %copy-done.14, ...), custom_call_target="tpu_custom_call" | custom-call | flops 60000002048 | bytes 2097152 | tf_op jit(solution)/shard_map/attend_others/pallas_call | solution.py:50
  56.4 1.9 %within.1.refs_2_ = f32[192,1024]{1,0:T(8,128)S(1)} custom-call(s32[4]{0:T(128)S(1)} %copy-done.18, bf16[192,1024]{1,0:T(8,128)(2,1)S(1)} %copy-done.3, f32[16,192]{1,0:T(8,128)S(1)} %bitcast.12, f32[192,16]{1,0:T(8,128)S(1)} %copy-done.5, f32[16,192]{1,0:T(8,128)S(1)} %get-tuple-element.14.refs_1_.refs_4_, ...), custom_call_target="tpu_custom_call" | custom-call | flops 150994944 | bytes 2097152 | tf_op jit(solution)/shard_map/within/pallas_call | solution.py:50
  59.1 0.9 %copy-done.8 = bf16[800,128]{1,0:T(8,128)(2,1)S(1)} copy-done((bf16[800,128]{1,0:T(8,128)(2,1)S(1)}, bf16[800,128]{1,0:T(8,128)(2,1)}, u32[]{:S(2)}) %copy-start.8) | copy-done | bytes 204824
  60.0 1.5 %scan.1 = bf16[32,64,128]{2,1,0:T(8,128)(2,1)} custom-call(s32[4]{0:T(128)S(1)} %copy-done.18, bf16[32,72,128]{2,1,0:T(8,128)(2,1)S(1)} %all-to-all-done.1.refs_1_, f32[192,1024]{1,0:T(8,128)S(1)} %within.1.refs_2_, bf16[800,128]{1,0:T(8,128)(2,1)S(1)} %copy-done.8), custom_call_target="tpu_custom_call" | custom-call | flops 1000000 | bytes 2097152 | tf_op jit(solution)/shard_map/scan/pallas_call | solution.py:50
  61.5 6.9 %all-to-all-start.2 = ((bf16[32,64,128]{2,1,0:T(8,128)(2,1)}), bf16[32,64,128]{2,1,0:T(8,128)(2,1)S(1)}, u32[]{:S(2)}, u32[]{:S(2)}) async-start(bf16[32,64,128]{2,1,0:T(8,128)(2,1)} %scan.1), calls=%async_computation.2 | async-start | bytes 1048576 | tf_op jit(solution)/shard_map/all_to_all | solution.py:450
  68.4 4.8 %collective-permute-start.6 = (bf16[800,128]{1,0:T(8,128)(2,1)}, bf16[800,128]{1,0:T(8,128)(2,1)S(1)}, u32[]{:S(2)}, u32[]{:S(2)}) collective-permute-start(bf16[800,128]{1,0:T(8,128)(2,1)} %copy-done.24), channel_id=1, source_target_pairs={{0,256},{128,384},{256,0},{384,128},{1,257},{129,385},{257,1},{385... | collective-permute-start | bytes 614408 | tf_op jit(solution)/shard_map/ppermute | solution.py:363
  73.2 2.2 %collective-permute-start.5 = (bf16[800,128]{1,0:T(8,128)(2,1)}, bf16[800,128]{1,0:T(8,128)(2,1)S(1)}, u32[]{:S(2)}, u32[]{:S(2)}) collective-permute-start(bf16[800,128]{1,0:T(8,128)(2,1)} %copy-done.10), channel_id=1, source_target_pairs={{0,128},{128,256},{256,384},{384,0},{1,129},{129,257},{257,385},{3... | collective-permute-start | bytes 614408 | tf_op jit(solution)/shard_map/ppermute | solution.py:363
  75.5 4.4 %collective-permute-start.4 = (bf16[800,128]{1,0:T(8,128)(2,1)S(1)}, bf16[800,128]{1,0:T(8,128)(2,1)S(1)}, u32[]{:S(2)}, u32[]{:S(2)}) collective-permute-start(bf16[800,128]{1,0:T(8,128)(2,1)S(1)} %copy-done.9), channel_id=1, source_target_pairs={{0,384},{128,0},{256,128},{384,256},{1,385},{129,1},{257,129},{385... | collective-permute-start | bytes 614408 | tf_op jit(solution)/shard_map/ppermute | solution.py:363
  79.9 1.1 %copy-done.23 = bf16[8,176,256]{2,1,0:T(8,128)(2,1)S(1)} copy-done((bf16[8,176,256]{2,1,0:T(8,128)(2,1)S(1)}, bf16[8,176,256]{2,1,0:T(8,128)(2,1)}, u32[]{:S(2)}) %copy-start.23) | copy-done | bytes 720920
  81.0 5.1 %attend_own.1.refs_1_ = bf16[800,128]{1,0:T(8,128)(2,1)S(1)} custom-call(s32[4]{0:T(128)S(1)} %copy-done.18, bf16[192,512]{1,0:T(8,128)(2,1)} %refs_1_.5, bf16[8,176,256]{2,1,0:T(8,128)(2,1)S(1)} %hold.2.refs_1_.refs_4_.refs_2_, bf16[8,176,256]{2,1,0:T(8,128)(2,1)S(1)} %copy-done.23), custom_call_target="tpu_custom_call" | custom-call | flops 1006632960 | bytes 2097152 | tf_op jit(solution)/shard_map/attend_own/pallas_call | solution.py:50
  86.2 2.0 %collective-permute-done.5.refs_3_ = bf16[800,128]{1,0:T(8,128)(2,1)S(1)} collective-permute-done((bf16[800,128]{1,0:T(8,128)(2,1)}, bf16[800,128]{1,0:T(8,128)(2,1)S(1)}, u32[]{:S(2)}, u32[]{:S(2)}) %collective-permute-start.5) | collective-permute-done | bytes 204832 | tf_op jit(solution)/shard_map/ppermute | solution.py:363
  88.1 1.9 %merge.1 = (bf16[192,512]{1,0:T(8,128)(2,1)}, bf16[192,1024]{1,0:T(8,128)(2,1)}, f32[1,1024]{1,0:T(1,128)}) custom-call(s32[4]{0:T(128)S(1)} %copy-done.18, bf16[800,128]{1,0:T(8,128)(2,1)S(1)} %attend_own.1.refs_1_, bf16[800,128]{1,0:T(8,128)(2,1)S(1)} %collective-permute-done.4.refs_2_, bf16[800,128]{1,0:T(8,128)(2,1)S(1)} %collective-permute-done.5.refs_3_, ...), custom_call_target="tpu_custom_call" | custom-call | flops 1000000 | bytes 2097152 | tf_op jit(solution)/shard_map/merge/pallas_call | solution.py:50
  90.1 1.9 %final.1 = bf16[192,1024]{1,0:T(8,128)(2,1)} custom-call(s32[4]{0:T(128)S(1)} %copy-done.18, bf16[32,64,128]{2,1,0:T(8,128)(2,1)S(1)} %all-to-all-done.2.refs_1_, f32[192,1024]{1,0:T(8,128)S(1)} %within.1.refs_2_, bf16[192,256]{1,0:T(8,128)(2,1)S(1)} %constant_dynamic-slice_fusion.refs_6_.refs_3_, f32[192,16]{1,0:T(8,128)S(1)} %copy-done.6), custom_call_target="tpu_custom_call" | custom-call | flops 100663296 | bytes 2097152 | tf_op jit(solution)/shard_map/final/pallas_call | solution.py:50
  (59 shorter events, 6.9 us)
Async XLA Ops:
  0.6 21.2 %copy-start = (bf16[192,2048]{1,0:T(8,128)(2,1)S(1)}, bf16[192,2048]{1,0:T(8,128)(2,1)}, u32[]{:S(2)}) copy-start(bf16[192,2048]{1,0:T(8,128)(2,1)} %param.15) | copy-start | bytes 2359300
  4.1 17.8 %copy-start.1 = (bf16[8,176,256]{2,1,0:T(8,128)(2,1)S(1)}, bf16[8,176,256]{2,1,0:T(8,128)(2,1)}, u32[]{:S(2)}) copy-start(bf16[8,176,256]{2,1,0:T(8,128)(2,1)} %pack.1.refs_6_) | copy-start | bytes 2162692
  4.1 17.8 %copy-start.3 = (bf16[192,1024]{1,0:T(8,128)(2,1)S(1)}, bf16[192,1024]{1,0:T(8,128)(2,1)}, u32[]{:S(2)}) copy-start(bf16[192,1024]{1,0:T(8,128)(2,1)} %refs_1_.4) | copy-start | bytes 1179652
  4.1 27.3 %all-to-all-start = ((bf16[8,176,256]{2,1,0:T(8,128)(2,1)}), bf16[8,176,256]{2,1,0:T(8,128)(2,1)S(1)}, u32[]{:S(2)}, u32[]{:S(2)}) async-start(bf16[8,176,256]{2,1,0:T(8,128)(2,1)} %pack.1.refs_6_), calls=%async_computation | async-start | bytes 1441792 | tf_op jit(solution)/shard_map/all_to_all | solution.py:399
  11.9 13.4 %collective-permute-start.1 = (bf16[192,512]{1,0:T(8,128)(2,1)}, bf16[192,512]{1,0:T(8,128)(2,1)S(1)}, u32[]{:S(2)}, u32[]{:S(2)}) collective-permute-start(bf16[192,512]{1,0:T(8,128)(2,1)} %refs_1_.5), channel_id=1, source_target_pairs={{0,384},{128,0},{256,128},{384,256},{1,385},{129,1},{257,129},{385... | collective-permute-start | bytes 589832 | tf_op jit(solution)/shard_map/ppermute | solution.py:363
  16.3 9.0 %collective-permute-start = (bf16[192,512]{1,0:T(8,128)(2,1)}, bf16[192,512]{1,0:T(8,128)(2,1)S(1)}, u32[]{:S(2)}, u32[]{:S(2)}) collective-permute-start(bf16[192,512]{1,0:T(8,128)(2,1)} %refs_1_.5), channel_id=1, source_target_pairs={{0,128},{128,256},{256,384},{384,0},{1,129},{129,257},{257,385},{3... | collective-permute-start | bytes 589832 | tf_op jit(solution)/shard_map/ppermute | solution.py:363
  18.2 9.8 %collective-permute-start.2 = (bf16[192,512]{1,0:T(8,128)(2,1)}, bf16[192,512]{1,0:T(8,128)(2,1)S(1)}, u32[]{:S(2)}, u32[]{:S(2)}) collective-permute-start(bf16[192,512]{1,0:T(8,128)(2,1)} %refs_1_.5), channel_id=1, source_target_pairs={{0,256},{128,384},{256,0},{384,128},{1,257},{129,385},{257,1},{385... | collective-permute-start | bytes 589832 | tf_op jit(solution)/shard_map/ppermute | solution.py:363
  25.3 6.1 %copy-start.4 = (f32[192,16]{1,0:T(8,128)}, f32[192,16]{1,0:T(8,128)S(1)}, u32[]{:S(2)}) copy-start(f32[192,16]{1,0:T(8,128)S(1)} %get-tuple-element.15.refs_3_.refs_4_) | copy-start | bytes 36868
  25.3 6.1 %copy-start.11 = (bf16[192,512]{1,0:T(8,128)(2,1)}, bf16[192,512]{1,0:T(8,128)(2,1)S(1)}, u32[]{:S(2)}) copy-start(bf16[192,512]{1,0:T(8,128)(2,1)S(1)} %collective-permute-done.1.refs_3_.refs_1_) | copy-start | bytes 589828
  25.3 6.1 %copy-start.13 = (bf16[192,512]{1,0:T(8,128)(2,1)}, bf16[192,512]{1,0:T(8,128)(2,1)S(1)}, u32[]{:S(2)}) copy-start(bf16[192,512]{1,0:T(8,128)(2,1)S(1)} %collective-permute-done.refs_2_.refs_3_) | copy-start | bytes 589828
  28.0 3.4 %copy-start.15 = (bf16[192,512]{1,0:T(8,128)(2,1)}, bf16[192,512]{1,0:T(8,128)(2,1)S(1)}, u32[]{:S(2)}) copy-start(bf16[192,512]{1,0:T(8,128)(2,1)S(1)} %collective-permute-done.2.refs_4_.refs_2_) | copy-start | bytes 589828
  31.4 10.8 %collective-permute-start.3 = (bf16[8,176,256]{2,1,0:T(8,128)(2,1)S(1)}, bf16[8,176,256]{2,1,0:T(8,128)(2,1)S(1)}, u32[]{:S(2)}, u32[]{:S(2)}) collective-permute-start(bf16[8,176,256]{2,1,0:T(8,128)(2,1)S(1)} %hold.2.refs_1_.refs_4_.refs_2_), channel_id=1, source_target_pairs={{0,1},{1,0},{2,3},{3,2},{4,5},{5,4},{6,7},{7,6},{8,9},{9,8},{10,11... | collective-permute-start | bytes 2162696 | tf_op jit(solution)/shard_map/ppermute | solution.py:426
  37.4 21.6 %all-to-all-start.1 = ((bf16[32,72,128]{2,1,0:T(8,128)(2,1)}), bf16[32,72,128]{2,1,0:T(8,128)(2,1)S(1)}, u32[]{:S(2)}, u32[]{:S(2)}) async-start(bf16[32,72,128]{2,1,0:T(8,128)(2,1)} %hold.3), calls=%async_computation.1 | async-start | bytes 1179648 | tf_op jit(solution)/shard_map/all_to_all | solution.py:429
  42.3 13.5 %copy-start.5 = (f32[192,16]{1,0:T(8,128)S(1)}, f32[192,16]{1,0:T(8,128)}, u32[]{:S(2)}) copy-start(f32[192,16]{1,0:T(8,128)} %copy-done.4) | copy-start | bytes 36868
  42.3 1.0 %copy-start.12 = (bf16[192,512]{1,0:T(8,128)(2,1)S(1)}, bf16[192,512]{1,0:T(8,128)(2,1)}, u32[]{:S(2)}) copy-start(bf16[192,512]{1,0:T(8,128)(2,1)} %copy-done.11) | copy-start | bytes 589828
  45.1 9.3 %copy-start.22 = (bf16[8,176,256]{2,1,0:T(8,128)(2,1)}, bf16[8,176,256]{2,1,0:T(8,128)(2,1)S(1)}, u32[]{:S(2)}) copy-start(bf16[8,176,256]{2,1,0:T(8,128)(2,1)S(1)} %collective-permute-done.3.refs_5_.refs_3_) | copy-start | bytes 2162692
  61.5 14.0 %copy-start.9 = (bf16[800,128]{1,0:T(8,128)(2,1)S(1)}, bf16[800,128]{1,0:T(8,128)(2,1)}, u32[]{:S(2)}) copy-start(bf16[800,128]{1,0:T(8,128)(2,1)} %copy-done.7) | copy-start | bytes 614404
  61.5 28.6 %all-to-all-start.2 = ((bf16[32,64,128]{2,1,0:T(8,128)(2,1)}), bf16[32,64,128]{2,1,0:T(8,128)(2,1)S(1)}, u32[]{:S(2)}, u32[]{:S(2)}) async-start(bf16[32,64,128]{2,1,0:T(8,128)(2,1)} %scan.1), calls=%async_computation.2 | async-start | bytes 1048576 | tf_op jit(solution)/shard_map/all_to_all | solution.py:450
  68.4 19.7 %copy-start.2 = (bf16[192,1024]{1,0:T(8,128)(2,1)S(1)}, bf16[192,1024]{1,0:T(8,128)(2,1)}, u32[]{:S(2)}) copy-start(bf16[192,1024]{1,0:T(8,128)(2,1)} %refs_5_.1) | copy-start | bytes 1179652
  68.4 17.7 %collective-permute-start.6 = (bf16[800,128]{1,0:T(8,128)(2,1)}, bf16[800,128]{1,0:T(8,128)(2,1)S(1)}, u32[]{:S(2)}, u32[]{:S(2)}) collective-permute-start(bf16[800,128]{1,0:T(8,128)(2,1)} %copy-done.24), channel_id=1, source_target_pairs={{0,256},{128,384},{256,0},{384,128},{1,257},{129,385},{257,1},{385... | collective-permute-start | bytes 614408 | tf_op jit(solution)/shard_map/ppermute | solution.py:363
  73.2 14.9 %collective-permute-start.5 = (bf16[800,128]{1,0:T(8,128)(2,1)}, bf16[800,128]{1,0:T(8,128)(2,1)S(1)}, u32[]{:S(2)}, u32[]{:S(2)}) collective-permute-start(bf16[800,128]{1,0:T(8,128)(2,1)} %copy-done.10), channel_id=1, source_target_pairs={{0,128},{128,256},{256,384},{384,0},{1,129},{129,257},{257,385},{3... | collective-permute-start | bytes 614408 | tf_op jit(solution)/shard_map/ppermute | solution.py:363
  75.5 12.6 %collective-permute-start.4 = (bf16[800,128]{1,0:T(8,128)(2,1)S(1)}, bf16[800,128]{1,0:T(8,128)(2,1)S(1)}, u32[]{:S(2)}, u32[]{:S(2)}) collective-permute-start(bf16[800,128]{1,0:T(8,128)(2,1)S(1)} %copy-done.9), channel_id=1, source_target_pairs={{0,384},{128,0},{256,128},{384,256},{1,385},{129,1},{257,129},{385... | collective-permute-start | bytes 614408 | tf_op jit(solution)/shard_map/ppermute | solution.py:363
  79.9 1.1 %copy-start.23 = (bf16[8,176,256]{2,1,0:T(8,128)(2,1)S(1)}, bf16[8,176,256]{2,1,0:T(8,128)(2,1)}, u32[]{:S(2)}) copy-start(bf16[8,176,256]{2,1,0:T(8,128)(2,1)} %copy-done.22) | copy-start | bytes 2162692
  86.1 3.9 %copy-start.6 = (f32[192,16]{1,0:T(8,128)S(1)}, f32[192,16]{1,0:T(8,128)}, u32[]{:S(2)}) copy-start(f32[192,16]{1,0:T(8,128)} %copy-done.4) | copy-start | bytes 36868
  (11 other events, 8.3 us)

commit v4 on v3

--- a/solution.py
+++ b/solution.py
@@ -445,7 +445,7 @@
         (place, recv),
         "scan",
         1000000,
-        after=(base, p_left),
+        after=(base,),
     )
     carried = lax.all_to_all(back, SEQ, 0, 0, tiled=True)
 
@@ -459,7 +459,7 @@
             jax.ShapeDtypeStruct((TOK, KV_HEADS * ATT_DIM), BF16),
             jax.ShapeDtypeStruct((1, KV_HEADS * ATT_DIM), F32),
         ],
-        (place, p_own, r_left, r_right, r_far, new_keys),
+        (place, p_own, r_far, r_right, r_left, new_keys),
         "merge",
         1000000,
     )

time: 92.8 us -> 91.5 us (0.986)
  local copies, waits for them, and re-layouts: 9.2 us -> 4.36 us
  waiting for transfers between devices: 8.09 us -> 11 us
  Pallas kernels: 27 us -> 28 us
    unnamed x50 -> x44, local copies, waits for them, and re-layouts: 8.27 us -> 3.43 us
    ppermute x6, waiting for transfers between devices: 4.68 us -> 6.38 us  [shift(): lax.ppermute(value, axis, [(i, (i + by) % size) for i in range(size)])]
    all_to_all x1, waiting for transfers between devices: 0.01 us -> 1.23 us  [body(): recv = lax.all_to_all(send, SEQ, 0, 0, tiled=True)]
    ppermute x6, starting transfers between devices: 21.4 us -> 20.2 us  [shift(): lax.ppermute(value, axis, [(i, (i + by) % size) for i in range(size)])]
    pallas_call x7, Pallas kernels: 24.3 us -> 25.2 us  [call(): pl.pallas_call(inner, out_shape=out_shape, in_specs=[pl.BlockSpec(memory_...]
  transfers between devices with their start and end apart: 10 -> 10, of which waited for: 3 -> 5; matrix products, arithmetic and copies ran while one was open for 1% -> 1% of each run, Pallas kernels for 23% -> 24%
where the time goes in v4:
time: 91.5 us; the launch traced here: 90.7 us
  starting transfers between devices  45.8 us (50%)
  Pallas kernels  28 us (31%)
  waiting for transfers between devices  11 us (12%)
  local copies, waits for them, and re-layouts  4.36 us (5%)
  between operations  0.96 us (1%)
    pallas_call x7, Pallas kernels, call(): pl.pallas_call(inner, out_shape=out_shape, in_specs=[pl.BlockSpec(memory_...  25.2 us
    ppermute x6, starting transfers between devices, shift(): lax.ppermute(value, axis, [(i, (i + by) % size) for i in range(size)])  20.2 us
    all_to_all x1, starting transfers between devices, body(): carried = lax.all_to_all(back, SEQ, 0, 0, tiled=True)  7.79 us
    all_to_all x1, starting transfers between devices, body(): kv_a = lax.all_to_all(packed, 'seq_1', 0, 0, tiled=True)  7.78 us
    ppermute x6, waiting for transfers between devices, shift(): lax.ppermute(value, axis, [(i, (i + by) % size) for i in range(size)])  6.38 us
    ppermute x1, starting transfers between devices, body(): kv_b = lax.ppermute(kv_a, 'head', swap)  5.09 us
    all_to_all x1, starting transfers between devices, body(): recv = lax.all_to_all(send, SEQ, 0, 0, tiled=True)  4.95 us
    unnamed x44, local copies, waits for them, and re-layouts  3.43 us
  transfers between devices with their start and end apart: 10, of which 5 were waited for; matrix products, arithmetic and copies ran while one was open for 1% of the time, Pallas kernels for 24%

profile of v4, /device:TPU:1, one launch (start us, length us, event | category | flops | bytes accessed | tf_op | source)
XLA Modules:
  0.0 90.7 jit_solution(9014668953419678481)
XLA Ops:
  1.3 2.8 %pack.1.refs_6_ = bf16[8,176,256]{2,1,0:T(8,128)(2,1)} custom-call(s32[4]{0:T(128)} %pad_add_fusion.place.refs_0_, bf16[128,1024]{1,0:T(8,128)(2,1)} %ck.1, bf16[128,1024]{1,0:T(8,128)(2,1)} %cv.1, bf16[192,1024]{1,0:T(8,128)(2,1)} %refs_5_.1, bf16[192,1024]{1,0:T(8,128)(2,1)} %nv.1, f32[1,1024]{1,0:T(1,128)} %bitcast.16, f32[1,1024]{1,0:T(1,128)} %bitcast.17, ...), custom_call_target="tpu_custom_call" | custom-call | flops 1000000 | bytes 2097152 | tf_op jit(solution)/shard_map/pack/pallas_call | solution.py:112
  4.1 7.8 %all-to-all-start = ((bf16[8,176,256]{2,1,0:T(8,128)(2,1)}), bf16[8,176,256]{2,1,0:T(8,128)(2,1)S(1)}, u32[]{:S(2)}, u32[]{:S(2)}) async-start(bf16[8,176,256]{2,1,0:T(8,128)(2,1)} %pack.1.refs_6_), calls=%async_computation | async-start | bytes 1441792 | tf_op jit(solution)/shard_map/all_to_all | solution.py:399
  11.9 4.4 %collective-permute-start.1 = (bf16[192,512]{1,0:T(8,128)(2,1)}, bf16[192,512]{1,0:T(8,128)(2,1)S(1)}, u32[]{:S(2)}, u32[]{:S(2)}) collective-permute-start(bf16[192,512]{1,0:T(8,128)(2,1)} %refs_1_.5), channel_id=1, source_target_pairs={{0,384},{128,0},{256,128},{384,256},{1,385},{129,1},{257,129},{385... | collective-permute-start | bytes 589832 | tf_op jit(solution)/shard_map/ppermute | solution.py:363
  16.3 1.9 %collective-permute-start = (bf16[192,512]{1,0:T(8,128)(2,1)}, bf16[192,512]{1,0:T(8,128)(2,1)S(1)}, u32[]{:S(2)}, u32[]{:S(2)}) collective-permute-start(bf16[192,512]{1,0:T(8,128)(2,1)} %refs_1_.5), channel_id=1, source_target_pairs={{0,128},{128,256},{256,384},{384,0},{1,129},{129,257},{257,385},{3... | collective-permute-start | bytes 589832 | tf_op jit(solution)/shard_map/ppermute | solution.py:363
  18.2 3.6 %collective-permute-start.2 = (bf16[192,512]{1,0:T(8,128)(2,1)}, bf16[192,512]{1,0:T(8,128)(2,1)S(1)}, u32[]{:S(2)}, u32[]{:S(2)}) collective-permute-start(bf16[192,512]{1,0:T(8,128)(2,1)} %refs_1_.5), channel_id=1, source_target_pairs={{0,256},{128,384},{256,0},{384,128},{1,257},{129,385},{257,1},{385... | collective-permute-start | bytes 589832 | tf_op jit(solution)/shard_map/ppermute | solution.py:363
  22.6 2.7 %local.1 = (bf16[32,72,128]{2,1,0:T(8,128)(2,1)}, f32[192,16]{1,0:T(8,128)S(1)}, f32[16,192]{1,0:T(8,128)S(1)}) custom-call(s32[4]{0:T(128)S(1)} %copy-done.16, bf16[192,1024]{1,0:T(8,128)(2,1)S(1)} %copy-done.3, f32[16,192]{1,0:T(8,128)S(1)} %bitcast.11, bf16[192,256]{1,0:T(8,128)(2,1)S(1)} %constant_dynamic-slice_fusion.1.refs_3_.refs_5_, ...), custom_call_target="tpu_custom_call" | custom-call | flops 100663296 | bytes 2097152 | tf_op jit(solution)/shard_map/local/pallas_call | solution.py:50
  25.3 2.7 %collective-permute-done.2.refs_4_.refs_2_ = bf16[192,512]{1,0:T(8,128)(2,1)S(1)} collective-permute-done((bf16[192,512]{1,0:T(8,128)(2,1)}, bf16[192,512]{1,0:T(8,128)(2,1)S(1)}, u32[]{:S(2)}, u32[]{:S(2)}) %collective-permute-start.2) | collective-permute-done | bytes 196640 | tf_op jit(solution)/shard_map/ppermute | solution.py:363
  28.0 3.4 %all-to-all-done.refs_0_ = bf16[8,176,256]{2,1,0:T(8,128)(2,1)S(1)} async-done(((bf16[8,176,256]{2,1,0:T(8,128)(2,1)}), bf16[8,176,256]{2,1,0:T(8,128)(2,1)S(1)}, u32[]{:S(2)}, u32[]{:S(2)}) %all-to-all-start) | async-done | bytes 720928 | tf_op jit(solution)/shard_map/all_to_all | solution.py:399
  31.4 5.1 %collective-permute-start.3 = (bf16[8,176,256]{2,1,0:T(8,128)(2,1)S(1)}, bf16[8,176,256]{2,1,0:T(8,128)(2,1)}, u32[]{:S(2)}, u32[]{:S(2)}) collective-permute-start(bf16[8,176,256]{2,1,0:T(8,128)(2,1)S(1)} %hold.2.refs_1_.refs_4_.refs_2_), channel_id=1, source_target_pairs={{0,1},{1,0},{2,3},{3,2},{4,5},{5,4},{6,7},{7,6},{8,9},{9,8},{10,11... | collective-permute-start | bytes 2162696 | tf_op jit(solution)/shard_map/ppermute | solution.py:426
  36.5 0.9 constant_dynamic-slice_fusion.refs_6_.refs_3_
  37.5 5.0 %all-to-all-start.1 = ((bf16[32,72,128]{2,1,0:T(8,128)(2,1)}), bf16[32,72,128]{2,1,0:T(8,128)(2,1)S(1)}, u32[]{:S(2)}, u32[]{:S(2)}) async-start(bf16[32,72,128]{2,1,0:T(8,128)(2,1)} %hold.3), calls=%async_computation.1 | async-start | bytes 1179648 | tf_op jit(solution)/shard_map/all_to_all | solution.py:429
  42.5 9.9 %attend_others.1 = (bf16[800,128]{1,0:T(8,128)(2,1)S(1)}, bf16[800,128]{1,0:T(8,128)(2,1)S(1)}, bf16[800,128]{1,0:T(8,128)(2,1)S(1)}) custom-call(s32[4]{0:T(128)S(1)} %copy-done.16, bf16[192,512]{1,0:T(8,128)(2,1)S(1)} %copy-done.10, bf16[192,512]{1,0:T(8,128)(2,1)S(1)} %copy-done.14, bf16[192,512]{1,0:T(8,128)(2,1)S(1)} %copy-done.12, ...), custom_call_target="tpu_custom_call" | custom-call | flops 60000002048 | bytes 2097152 | tf_op jit(solution)/shard_map/attend_others/pallas_call | solution.py:50
  54.4 2.0 %within.1.refs_2_ = f32[192,1024]{1,0:T(8,128)S(1)} custom-call(s32[4]{0:T(128)S(1)} %copy-done.16, bf16[192,1024]{1,0:T(8,128)(2,1)S(1)} %copy-done.3, f32[16,192]{1,0:T(8,128)S(1)} %bitcast.12, f32[192,16]{1,0:T(8,128)S(1)} %copy-done.5, f32[16,192]{1,0:T(8,128)S(1)} %get-tuple-element.14.refs_1_.refs_4_, ...), custom_call_target="tpu_custom_call" | custom-call | flops 150994944 | bytes 2097152 | tf_op jit(solution)/shard_map/within/pallas_call | solution.py:50
  57.0 1.2 %all-to-all-done.1.refs_1_ = bf16[32,72,128]{2,1,0:T(8,128)(2,1)S(1)} async-done(((bf16[32,72,128]{2,1,0:T(8,128)(2,1)}), bf16[32,72,128]{2,1,0:T(8,128)(2,1)S(1)}, u32[]{:S(2)}, u32[]{:S(2)}) %all-to-all-start.1) | async-done | bytes 589856 | tf_op jit(solution)/shard_map/all_to_all | solution.py:429
  58.3 1.5 %scan.1 = bf16[32,64,128]{2,1,0:T(8,128)(2,1)} custom-call(s32[4]{0:T(128)S(1)} %copy-done.16, bf16[32,72,128]{2,1,0:T(8,128)(2,1)S(1)} %all-to-all-done.1.refs_1_, f32[192,1024]{1,0:T(8,128)S(1)} %within.1.refs_2_), custom_call_target="tpu_custom_call" | custom-call | flops 1000000 | bytes 2097152 | tf_op jit(solution)/shard_map/scan/pallas_call | solution.py:50
  59.7 7.8 %all-to-all-start.2 = ((bf16[32,64,128]{2,1,0:T(8,128)(2,1)}), bf16[32,64,128]{2,1,0:T(8,128)(2,1)S(1)}, u32[]{:S(2)}, u32[]{:S(2)}) async-start(bf16[32,64,128]{2,1,0:T(8,128)(2,1)} %scan.1), calls=%async_computation.2 | async-start | bytes 1048576 | tf_op jit(solution)/shard_map/all_to_all | solution.py:450
  67.5 4.6 %collective-permute-start.4 = (bf16[800,128]{1,0:T(8,128)(2,1)}, bf16[800,128]{1,0:T(8,128)(2,1)S(1)}, u32[]{:S(2)}, u32[]{:S(2)}) collective-permute-start(bf16[800,128]{1,0:T(8,128)(2,1)} %copy-done.21), channel_id=1, source_target_pairs={{0,256},{128,384},{256,0},{384,128},{1,257},{129,385},{257,1},{385... | collective-permute-start | bytes 614408 | tf_op jit(solution)/shard_map/ppermute | solution.py:363
  72.2 2.9 %collective-permute-start.6 = (bf16[800,128]{1,0:T(8,128)(2,1)}, bf16[800,128]{1,0:T(8,128)(2,1)S(1)}, u32[]{:S(2)}, u32[]{:S(2)}) collective-permute-start(bf16[800,128]{1,0:T(8,128)(2,1)} %copy-done.20), channel_id=1, source_target_pairs={{0,384},{128,0},{256,128},{384,256},{1,385},{129,1},{257,129},{385... | collective-permute-start | bytes 614408 | tf_op jit(solution)/shard_map/ppermute | solution.py:363
  75.1 2.7 %collective-permute-start.5 = (bf16[800,128]{1,0:T(8,128)(2,1)S(1)}, bf16[800,128]{1,0:T(8,128)(2,1)S(1)}, u32[]{:S(2)}, u32[]{:S(2)}) collective-permute-start(bf16[800,128]{1,0:T(8,128)(2,1)S(1)} %copy-done.8), channel_id=1, source_target_pairs={{0,128},{128,256},{256,384},{384,0},{1,129},{129,257},{257,385},{3... | collective-permute-start | bytes 614408 | tf_op jit(solution)/shard_map/ppermute | solution.py:363
  77.8 5.4 %attend_own.1.refs_1_ = bf16[800,128]{1,0:T(8,128)(2,1)S(1)} custom-call(s32[4]{0:T(128)S(1)} %copy-done.16, bf16[192,512]{1,0:T(8,128)(2,1)} %refs_1_.5, bf16[8,176,256]{2,1,0:T(8,128)(2,1)S(1)} %hold.2.refs_1_.refs_4_.refs_2_, bf16[8,176,256]{2,1,0:T(8,128)(2,1)} %collective-permute-done.3.refs_5_.refs_3_), custom_call_target="tpu_custom_call" | custom-call | flops 1006632960 | bytes 2097152 | tf_op jit(solution)/shard_map/attend_own/pallas_call | solution.py:50
  83.2 2.7 %collective-permute-done.6.refs_4_ = bf16[800,128]{1,0:T(8,128)(2,1)S(1)} collective-permute-done((bf16[800,128]{1,0:T(8,128)(2,1)}, bf16[800,128]{1,0:T(8,128)(2,1)S(1)}, u32[]{:S(2)}, u32[]{:S(2)}) %collective-permute-start.6) | collective-permute-done | bytes 204832 | tf_op jit(solution)/shard_map/ppermute | solution.py:363
  85.9 1.0 %collective-permute-done.5.refs_3_ = bf16[800,128]{1,0:T(8,128)(2,1)S(1)} collective-permute-done((bf16[800,128]{1,0:T(8,128)(2,1)S(1)}, bf16[800,128]{1,0:T(8,128)(2,1)S(1)}, u32[]{:S(2)}, u32[]{:S(2)}) %collective-permute-start.5) | collective-permute-done | bytes 204832 | tf_op jit(solution)/shard_map/ppermute | solution.py:363
  86.9 1.9 %merge.1 = (bf16[192,512]{1,0:T(8,128)(2,1)}, bf16[192,1024]{1,0:T(8,128)(2,1)}, f32[1,1024]{1,0:T(1,128)}) custom-call(s32[4]{0:T(128)S(1)} %copy-done.16, bf16[800,128]{1,0:T(8,128)(2,1)S(1)} %attend_own.1.refs_1_, bf16[800,128]{1,0:T(8,128)(2,1)S(1)} %collective-permute-done.4.refs_2_, bf16[800,128]{1,0:T(8,128)(2,1)S(1)} %collective-permute-done.5.refs_3_, ...), custom_call_target="tpu_custom_call" | custom-call | flops 1000000 | bytes 2097152 | tf_op jit(solution)/shard_map/merge/pallas_call | solution.py:50
  88.9 1.9 %final.1 = bf16[192,1024]{1,0:T(8,128)(2,1)} custom-call(s32[4]{0:T(128)S(1)} %copy-done.16, bf16[32,64,128]{2,1,0:T(8,128)(2,1)S(1)} %all-to-all-done.2.refs_1_, f32[192,1024]{1,0:T(8,128)S(1)} %within.1.refs_2_, bf16[192,256]{1,0:T(8,128)(2,1)S(1)} %constant_dynamic-slice_fusion.refs_6_.refs_3_, f32[192,16]{1,0:T(8,128)S(1)} %copy-done.6), custom_call_target="tpu_custom_call" | custom-call | flops 100663296 | bytes 2097152 | tf_op jit(solution)/shard_map/final/pallas_call | solution.py:50
  (53 shorter events, 4.1 us)
Async XLA Ops:
  0.6 21.2 %copy-start = (bf16[192,2048]{1,0:T(8,128)(2,1)S(1)}, bf16[192,2048]{1,0:T(8,128)(2,1)}, u32[]{:S(2)}) copy-start(bf16[192,2048]{1,0:T(8,128)(2,1)} %param.15) | copy-start | bytes 2359300
  4.1 17.8 %copy-start.1 = (bf16[8,176,256]{2,1,0:T(8,128)(2,1)S(1)}, bf16[8,176,256]{2,1,0:T(8,128)(2,1)}, u32[]{:S(2)}) copy-start(bf16[8,176,256]{2,1,0:T(8,128)(2,1)} %pack.1.refs_6_) | copy-start | bytes 2162692
  4.1 17.8 %copy-start.3 = (bf16[192,1024]{1,0:T(8,128)(2,1)S(1)}, bf16[192,1024]{1,0:T(8,128)(2,1)}, u32[]{:S(2)}) copy-start(bf16[192,1024]{1,0:T(8,128)(2,1)} %refs_1_.4) | copy-start | bytes 1179652
  4.1 27.3 %all-to-all-start = ((bf16[8,176,256]{2,1,0:T(8,128)(2,1)}), bf16[8,176,256]{2,1,0:T(8,128)(2,1)S(1)}, u32[]{:S(2)}, u32[]{:S(2)}) async-start(bf16[8,176,256]{2,1,0:T(8,128)(2,1)} %pack.1.refs_6_), calls=%async_computation | async-start | bytes 1441792 | tf_op jit(solution)/shard_map/all_to_all | solution.py:399
  11.9 13.4 %collective-permute-start.1 = (bf16[192,512]{1,0:T(8,128)(2,1)}, bf16[192,512]{1,0:T(8,128)(2,1)S(1)}, u32[]{:S(2)}, u32[]{:S(2)}) collective-permute-start(bf16[192,512]{1,0:T(8,128)(2,1)} %refs_1_.5), channel_id=1, source_target_pairs={{0,384},{128,0},{256,128},{384,256},{1,385},{129,1},{257,129},{385... | collective-permute-start | bytes 589832 | tf_op jit(solution)/shard_map/ppermute | solution.py:363
  16.3 9.0 %collective-permute-start = (bf16[192,512]{1,0:T(8,128)(2,1)}, bf16[192,512]{1,0:T(8,128)(2,1)S(1)}, u32[]{:S(2)}, u32[]{:S(2)}) collective-permute-start(bf16[192,512]{1,0:T(8,128)(2,1)} %refs_1_.5), channel_id=1, source_target_pairs={{0,128},{128,256},{256,384},{384,0},{1,129},{129,257},{257,385},{3... | collective-permute-start | bytes 589832 | tf_op jit(solution)/shard_map/ppermute | solution.py:363
  18.2 9.8 %collective-permute-start.2 = (bf16[192,512]{1,0:T(8,128)(2,1)}, bf16[192,512]{1,0:T(8,128)(2,1)S(1)}, u32[]{:S(2)}, u32[]{:S(2)}) collective-permute-start(bf16[192,512]{1,0:T(8,128)(2,1)} %refs_1_.5), channel_id=1, source_target_pairs={{0,256},{128,384},{256,0},{384,128},{1,257},{129,385},{257,1},{385... | collective-permute-start | bytes 589832 | tf_op jit(solution)/shard_map/ppermute | solution.py:363
  25.3 6.1 %copy-start.4 = (f32[192,16]{1,0:T(8,128)}, f32[192,16]{1,0:T(8,128)S(1)}, u32[]{:S(2)}) copy-start(f32[192,16]{1,0:T(8,128)S(1)} %get-tuple-element.15.refs_3_.refs_4_) | copy-start | bytes 36868
  25.3 6.1 %copy-start.9 = (bf16[192,512]{1,0:T(8,128)(2,1)}, bf16[192,512]{1,0:T(8,128)(2,1)S(1)}, u32[]{:S(2)}) copy-start(bf16[192,512]{1,0:T(8,128)(2,1)S(1)} %collective-permute-done.1.refs_3_.refs_1_) | copy-start | bytes 589828
  25.3 6.1 %copy-start.11 = (bf16[192,512]{1,0:T(8,128)(2,1)}, bf16[192,512]{1,0:T(8,128)(2,1)S(1)}, u32[]{:S(2)}) copy-start(bf16[192,512]{1,0:T(8,128)(2,1)S(1)} %collective-permute-done.refs_2_.refs_3_) | copy-start | bytes 589828
  28.0 3.4 %copy-start.13 = (bf16[192,512]{1,0:T(8,128)(2,1)}, bf16[192,512]{1,0:T(8,128)(2,1)S(1)}, u32[]{:S(2)}) copy-start(bf16[192,512]{1,0:T(8,128)(2,1)S(1)} %collective-permute-done.2.refs_4_.refs_2_) | copy-start | bytes 589828
  31.4 11.0 %collective-permute-start.3 = (bf16[8,176,256]{2,1,0:T(8,128)(2,1)S(1)}, bf16[8,176,256]{2,1,0:T(8,128)(2,1)}, u32[]{:S(2)}, u32[]{:S(2)}) collective-permute-start(bf16[8,176,256]{2,1,0:T(8,128)(2,1)S(1)} %hold.2.refs_1_.refs_4_.refs_2_), channel_id=1, source_target_pairs={{0,1},{1,0},{2,3},{3,2},{4,5},{5,4},{6,7},{7,6},{8,9},{9,8},{10,11... | collective-permute-start | bytes 2162696 | tf_op jit(solution)/shard_map/ppermute | solution.py:426
  37.4 5.0 %copy-start.10 = (bf16[192,512]{1,0:T(8,128)(2,1)S(1)}, bf16[192,512]{1,0:T(8,128)(2,1)}, u32[]{:S(2)}) copy-start(bf16[192,512]{1,0:T(8,128)(2,1)} %copy-done.9) | copy-start | bytes 589828
  37.4 5.0 %copy-start.12 = (bf16[192,512]{1,0:T(8,128)(2,1)S(1)}, bf16[192,512]{1,0:T(8,128)(2,1)}, u32[]{:S(2)}) copy-start(bf16[192,512]{1,0:T(8,128)(2,1)} %copy-done.11) | copy-start | bytes 589828
  37.4 5.0 %copy-start.14 = (bf16[192,512]{1,0:T(8,128)(2,1)S(1)}, bf16[192,512]{1,0:T(8,128)(2,1)}, u32[]{:S(2)}) copy-start(bf16[192,512]{1,0:T(8,128)(2,1)} %copy-done.13) | copy-start | bytes 589828
  37.5 20.8 %all-to-all-start.1 = ((bf16[32,72,128]{2,1,0:T(8,128)(2,1)}), bf16[32,72,128]{2,1,0:T(8,128)(2,1)S(1)}, u32[]{:S(2)}, u32[]{:S(2)}) async-start(bf16[32,72,128]{2,1,0:T(8,128)(2,1)} %hold.3), calls=%async_computation.1 | async-start | bytes 1179648 | tf_op jit(solution)/shard_map/all_to_all | solution.py:429
  42.4 11.3 %copy-start.5 = (f32[192,16]{1,0:T(8,128)S(1)}, f32[192,16]{1,0:T(8,128)}, u32[]{:S(2)}) copy-start(f32[192,16]{1,0:T(8,128)} %copy-done.4) | copy-start | bytes 36868
  59.7 15.4 %copy-start.8 = (bf16[800,128]{1,0:T(8,128)(2,1)S(1)}, bf16[800,128]{1,0:T(8,128)(2,1)}, u32[]{:S(2)}) copy-start(bf16[800,128]{1,0:T(8,128)(2,1)} %copy-done.7) | copy-start | bytes 614404
  59.7 29.1 %all-to-all-start.2 = ((bf16[32,64,128]{2,1,0:T(8,128)(2,1)}), bf16[32,64,128]{2,1,0:T(8,128)(2,1)S(1)}, u32[]{:S(2)}, u32[]{:S(2)}) async-start(bf16[32,64,128]{2,1,0:T(8,128)(2,1)} %scan.1), calls=%async_computation.2 | async-start | bytes 1048576 | tf_op jit(solution)/shard_map/all_to_all | solution.py:450
  67.5 15.7 %collective-permute-start.4 = (bf16[800,128]{1,0:T(8,128)(2,1)}, bf16[800,128]{1,0:T(8,128)(2,1)S(1)}, u32[]{:S(2)}, u32[]{:S(2)}) collective-permute-start(bf16[800,128]{1,0:T(8,128)(2,1)} %copy-done.21), channel_id=1, source_target_pairs={{0,256},{128,384},{256,0},{384,128},{1,257},{129,385},{257,1},{385... | collective-permute-start | bytes 614408 | tf_op jit(solution)/shard_map/ppermute | solution.py:363
  72.2 14.7 %copy-start.2 = (bf16[192,1024]{1,0:T(8,128)(2,1)S(1)}, bf16[192,1024]{1,0:T(8,128)(2,1)}, u32[]{:S(2)}) copy-start(bf16[192,1024]{1,0:T(8,128)(2,1)} %refs_5_.1) | copy-start | bytes 1179652
  72.2 13.7 %collective-permute-start.6 = (bf16[800,128]{1,0:T(8,128)(2,1)}, bf16[800,128]{1,0:T(8,128)(2,1)S(1)}, u32[]{:S(2)}, u32[]{:S(2)}) collective-permute-start(bf16[800,128]{1,0:T(8,128)(2,1)} %copy-done.20), channel_id=1, source_target_pairs={{0,384},{128,0},{256,128},{384,256},{1,385},{129,1},{257,129},{385... | collective-permute-start | bytes 614408 | tf_op jit(solution)/shard_map/ppermute | solution.py:363
  75.1 11.8 %collective-permute-start.5 = (bf16[800,128]{1,0:T(8,128)(2,1)S(1)}, bf16[800,128]{1,0:T(8,128)(2,1)S(1)}, u32[]{:S(2)}, u32[]{:S(2)}) collective-permute-start(bf16[800,128]{1,0:T(8,128)(2,1)S(1)} %copy-done.8), channel_id=1, source_target_pairs={{0,128},{128,256},{256,384},{384,0},{1,129},{129,257},{257,385},{3... | collective-permute-start | bytes 614408 | tf_op jit(solution)/shard_map/ppermute | solution.py:363
  83.2 5.6 %copy-start.6 = (f32[192,16]{1,0:T(8,128)S(1)}, f32[192,16]{1,0:T(8,128)}, u32[]{:S(2)}) copy-start(f32[192,16]{1,0:T(8,128)} %copy-done.4) | copy-start | bytes 36868
  (8 other events, 5.5 us)
